TPU v7x, 256 devices: a whole 4x4x8 slice. The times are simulated.
256 devices in a mesh: dp: 16 (over x, y), mp: 16 (over z, core).
Axes of the slice: x: 4, y: 4, z: 8, core: 2. Of those that a mesh axis runs over, the one named last changes fastest.
Arguments:
- hidden_state: bfloat16 [256, 8192], P('dp'), may hold values from -60 to 60, as said below
- norm_gain: bfloat16 [8192], replicated, may hold values from 0.5 to 1.5
- critic_weight: bfloat16 [8192, 65536], P(None, ('dp', 'mp')), may hold values from -8 to 8
- policy_weight: bfloat16 [8192, 65536], P(None, ('dp', 'mp')), may hold values from -8 to 8
- value_weight: bfloat16 [8192], replicated, may hold values from -0.0625 to 0.0625
- actions: int32 [256], replicated, may hold values from 0 to 65535, as said below
- rewards: int32 [256], replicated, may hold values from -4 to 4
- done_flags: int32 [256], replicated, may hold values 0 or 1
- pad_mask: int32 [256], replicated, may hold values 0 or 1
Outputs:
- grad_hidden: bfloat16 [256, 8192], P(('dp', 'mp'))
- grad_gain: float32 [8192], replicated
- grad_critic: bfloat16 [8192, 65536], P(None, ('dp', 'mp'))
- grad_value: float32 [8192], replicated
Inputs may be any that keep to these rules, and one draw needn't show every extreme that they name: `hidden_state`: hidden states of the trunk. `actions`: about half of the tokens, chosen at random, take an id from the block of 4096 ids that lies half the vocabulary away from the block at the token's own relative position (token t's block is t * 65536 // 4096 // 256); the others take any id.
All inputs are finite; a program needn't handle non-finite values.
Results may differ from a plain program's by a relative error of at most 0.0015.
The roundings to bfloat16 on the way count: a program that leaves them out, or rounds other values in their place, can miss the bound.
Values may be sent and summed in bfloat16 or wider, within the bound.
No kernel may reach another device: no remote copies, remote signals or barrier semaphores. Data moves between devices by JAX's collectives and lax.ppermute only.
A program may use at most 128 MiB of HBM per device.

v0:
```python
import jax
import jax.numpy as jnp
from jax import lax
from jax.sharding import PartitionSpec as P

D = 8192


discount = 0.99
expectile = 0.7
conservative = 0.5
reward_step = 0.5
epsilon = 1e-05


def contract_rows(left_side, right_side):
    return lax.dot_general(
        left_side, right_side, (((1,), (1,)), ((), ())), preferred_element_type=jnp.float32
    )


def body(
    hidden_state,
    norm_gain,
    critic_weight,
    policy_weight,
    value_weight,
    actions,
    rewards,
    done_flags,
    pad_mask,
):
    state_float = hidden_state.astype(jnp.float32)
    row_inverse = lax.rsqrt(jnp.mean(state_float * state_float, axis=1) + epsilon)
    unit_state = state_float * row_inverse[:, None]
    gain_float = norm_gain.astype(jnp.float32)
    normed_own = (unit_state * gain_float[None, :]).astype(jnp.bfloat16)
    portion = lax.all_gather(normed_own, "dp", axis=0, tiled=True)
    critic_logits = jnp.dot(portion, critic_weight, preferred_element_type=jnp.float32)
    policy_logits = jnp.dot(portion, policy_weight, preferred_element_type=jnp.float32)
    values = jnp.dot(portion, value_weight, preferred_element_type=jnp.float32)
    vocab_width = critic_weight.shape[1]
    block_index = lax.axis_index("dp") * lax.axis_size("mp") + lax.axis_index("mp")
    columns = block_index * vocab_width + jnp.arange(vocab_width, dtype=jnp.int32)
    chosen = (actions[:, None] == columns[None, :]).astype(jnp.float32)
    taken_part = jnp.sum(critic_logits * chosen, axis=1)
    critic_top = jnp.max(critic_logits, axis=1)
    policy_top = jnp.max(policy_logits, axis=1)
    critic_max, policy_max = lax.pmax((critic_top, policy_top), ("dp", "mp"))
    critic_total, policy_total, critic_taken = lax.psum(
        (
            jnp.sum(jnp.exp(critic_logits - critic_max[:, None]), axis=1),
            jnp.sum(jnp.exp(policy_logits - policy_max[:, None]), axis=1),
            taken_part,
        ),
        ("dp", "mp"),
    )
    critic_probs = jnp.exp(critic_logits - critic_max[:, None]) / critic_total[:, None]
    policy_probs = jnp.exp(policy_logits - policy_max[:, None]) / policy_total[:, None]
    next_values = jnp.concatenate([values[1:], jnp.zeros((1,), jnp.float32)])
    target = (
        reward_step * rewards.astype(jnp.float32)
        + discount * (1.0 - done_flags.astype(jnp.float32)) * next_values
    )
    live_mask = pad_mask.astype(jnp.float32)
    advantage = critic_taken - values
    weights = jnp.where(advantage >= 0.0, expectile, 1.0 - expectile)
    value_coef = live_mask * -2.0 * weights * advantage
    critic_coef = live_mask * (2.0 * (critic_taken - target) - conservative)
    critic_grad = (
        conservative * live_mask[:, None] * critic_probs + critic_coef[:, None] * chosen
    ).astype(jnp.bfloat16)
    policy_grad = (live_mask[:, None] * (policy_probs - chosen)).astype(jnp.bfloat16)
    grad_critic = lax.dot_general(
        portion, critic_grad, (((0,), (0,)), ((), ())), preferred_element_type=jnp.float32
    ).astype(jnp.bfloat16)
    grad_value = jnp.dot(
        value_coef, portion, precision=lax.Precision.HIGHEST, preferred_element_type=jnp.float32
    )
    own_rows = hidden_state.shape[0] // lax.axis_size("mp")
    normed_grad = lax.psum_scatter(
        contract_rows(critic_grad, critic_weight) + contract_rows(policy_grad, policy_weight),
        ("dp", "mp"),
        scatter_dimension=0,
        tiled=True,
    )
    own_start = block_index * own_rows
    own_coef = lax.dynamic_slice_in_dim(value_coef, own_start, own_rows, 0)
    normed_grad = normed_grad + own_coef[:, None] * value_weight.astype(jnp.float32)[None, :]
    local_start = lax.axis_index("mp") * own_rows
    own_unit = lax.dynamic_slice_in_dim(unit_state, local_start, own_rows, 0)
    own_inverse = lax.dynamic_slice_in_dim(row_inverse, local_start, own_rows, 0)
    scaled = normed_grad * gain_float[None, :]
    row_dot = jnp.sum(scaled * own_unit, axis=1)
    grad_hidden = (own_inverse[:, None] * (scaled - own_unit * row_dot[:, None] / D)).astype(
        jnp.bfloat16
    )
    grad_gain = lax.psum(jnp.sum(normed_grad * own_unit, axis=0), ("dp", "mp"))
    return (grad_hidden, grad_gain, grad_critic, grad_value)


def solution(mesh):
    placed = (
        P("dp", None),
        P(),
        P(None, ("dp", "mp")),
        P(None, ("dp", "mp")),
        P(),
        P(),
        P(),
        P(),
        P(),
    )
    return jax.shard_map(
        body,
        mesh=mesh,
        in_specs=placed,
        out_specs=(P(("dp", "mp"), None), P(), P(None, ("dp", "mp")), P()),
        check_vma=False,
    )
```

profile of v0, /device:TPU:1, one launch (start us, length us, event | category | flops | bytes accessed | tf_op | source)
XLA Modules:
  0.0 601.6 jit_solution(16940995521760465607)
XLA Ops:
  7.2 0.0 all-gather.2.cloned.1.call-start
  7.2 1.1 fusion
  8.3 0.7 convert_element_type.38
  9.1 1.8 multiply_convert_fusion
  10.9 0.0 all-gather.2.cloned.1.call-update
  10.9 0.0 all-reduce.5.cloned.1.call-start
  10.9 0.7 convert_element_type.37
  11.6 0.7 reshape.40
  12.4 59.0 %all-gather.2.cloned.1.call-done = bf16[256,8192]{1,0:T(8,128)(2,1)} async-done(((bf16[16,8192]{1,0:T(8,128)(2,1)}), bf16[256,8192]{1,0:T(8,128)(2,1)}) %all-gather.2.cloned.1.call-update) | async-done | bytes 4194320 | tf_op jit(solution)/shard_map/all_gather | solution.py:38
  71.4 0.0 copy-start
  71.4 3.5 fusion.27
  74.9 0.1 slice.3
  75.0 0.0 copy-done
  75.0 0.0 copy-start.2
  75.0 4.2 fusion.26
  79.2 0.0 copy-done.2
  79.2 0.0 copy-start.5
  79.2 0.0 copy-start.6
  79.2 0.0 copy-start.7
  79.3 0.0 copy-start.8
  79.3 1.8 fusion.25
  81.1 75.9 %all-reduce.2 = (f32[256]{0:T(256)S(1)}, f32[256]{0:T(256)S(1)}) all-reduce(f32[256]{0:T(256)S(1)} %get-tuple-element.19, f32[256]{0:T(256)S(1)} %get-tuple-element.21), channel_id=1, replica_groups=mesh['dp'=16,'mp'=16] {'dp','mp'}, use_global_device_ids=true, to_apply=%region_2.0 | all-reduce | flops 512 | bytes 4096 | tf_op jit(solution)/shard_map/pmax | solution.py:49
  157.1 0.0 copy-done.5
  157.1 0.1 fusion.7
  157.2 74.5 %all-reduce.1 = (f32[256]{0:T(256)S(1)}, f32[256]{0:T(256)S(1)}, f32[256]{0:T(256)S(1)}) all-reduce(f32[256]{0:T(256)S(1)} %get-tuple-element.5, f32[256]{0:T(256)S(1)} %get-tuple-element.4, f32[256]{0:T(256)S(1)} %get-tuple-element.23), channel_id=1, replica_groups=mesh['dp'=16,'mp'=16] {'dp','mp'}, use_global_device_ids=true, to_apply=%region_6.0 | all-reduce | flops 768 | bytes 6144 | tf_op jit(solution)/shard_map/psum | solution.py:50
  231.7 0.0 copy-done.6
  231.7 0.0 copy-done.7
  231.7 0.0 copy-done.8
  231.7 0.1 add_multiply_fusion
  231.8 0.0 copy-start.3
  231.8 3.7 fusion.22
  235.5 0.0 copy-done.3
  235.6 4.6 convolution_add_fusion
  240.2 0.0 copy-start.4
  240.2 0.0 all-reduce.5.cloned.1.call-update
  240.2 0.6 dynamic_slice.9
  240.8 0.0 copy-start.1
  240.8 0.6 dynamic_slice.10
  241.4 0.0 copy-done.4
  241.4 0.9 convert_multiply_fusion.2
  242.4 4.5 fusion.28
  246.9 0.0 copy-done.1
  246.9 3.4 convolution_convert_fusion
  250.3 263.3 %all-reduce.5.cloned.1.call-done = f32[256,8192]{1,0:T(8,128)} async-done(((f32[256,8192]{1,0:T(8,128)}), f32[256,8192]{1,0:T(8,128)}) %all-reduce.5.cloned.1.call-update) | async-done | bytes 8388624
  513.6 1.6 multiply_reduce_fusion
  515.2 77.6 %psum.31 = f32[8192]{0:T(1024)} all-reduce(f32[8192]{0:T(1024)S(1)} %bitcast.21), channel_id=1, replica_groups=mesh['dp'=16,'mp'=16] {'dp','mp'}, use_global_device_ids=true, to_apply=%region_13.14 | all-reduce | flops 8192 | bytes 65536 | tf_op jit(solution)/shard_map/psum | solution.py:98
  592.9 1.9 multiply_convert_fusion.1
  (2 shorter events, 0.0 us)
Async XLA Ops:
  7.2 64.2 %all-gather.2.cloned.1.call-start = ((), (), s32[]{:S(2)}) async-start(), calls=%async_computation | async-start | bytes 4456448 | tf_op jit(solution)/shard_map/all_gather | solution.py:38
  10.9 502.7 %all-reduce.5.cloned.1.call-start = ((), (), s32[]{:S(2)}) async-start(), calls=%async_computation.1 | async-start | bytes 16777216
  71.4 3.6 copy-start
  75.0 4.2 copy-start.2
  79.2 77.8 %copy-start.5 = (s32[256]{0:T(256)S(1)}, s32[256]{0:T(256)}, u32[]{:S(2)}) copy-start(s32[256]{0:T(256)} %param.14) | copy-start | bytes 3076
  79.2 152.5 %copy-start.6 = (s32[256]{0:T(256)S(1)}, s32[256]{0:T(256)}, u32[]{:S(2)}) copy-start(s32[256]{0:T(256)} %param.17) | copy-start | bytes 3076
  79.2 152.5 %copy-start.7 = (s32[256]{0:T(256)S(1)}, s32[256]{0:T(256)}, u32[]{:S(2)}) copy-start(s32[256]{0:T(256)} %param.16) | copy-start | bytes 3076
  79.3 152.5 %copy-start.8 = (s32[256]{0:T(256)S(1)}, s32[256]{0:T(256)}, u32[]{:S(2)}) copy-start(s32[256]{0:T(256)} %param.15) | copy-start | bytes 3076
  231.8 3.7 copy-start.3
  240.2 1.2 copy-start.4
  240.8 6.1 %copy-start.1 = (bf16[256,8192]{1,0:T(8,128)(2,1)S(1)}, bf16[256,8192]{1,0:T(8,128)(2,1)}, u32[]{:S(2)}) copy-start(bf16[256,8192]{1,0:T(8,128)(2,1)} %all-gather.2.cloned.1.call-done) | copy-start | bytes 12582916
Sparse Core Ops, SparseCore 0:
  11.0 60.3 all-gather.1
  240.3 273.2 all-reduce.4
where the time goes:
time: 602 us
  waiting for transfers between devices  322 us (53%)
  blocking collectives  228 us (38%)
  matrix products  25.9 us (4%)
  between operations  14.2 us (2%)
  other arithmetic  8.96 us (1%)
    unnamed x3, waiting for transfers between devices  263 us
    psum x1, blocking collectives, body(): grad_gain = lax.psum(jnp.sum(normed_grad * own_unit, axis=0), ('dp', 'mp'))  77.6 us
    pmax x1, blocking collectives, body(): critic_max, policy_max = lax.pmax((critic_top, policy_top), ('dp', 'mp'))  75.9 us
    psum x1, blocking collectives, body(): lax.psum((jnp.sum(jnp.exp(critic_logits - critic_max[:, None]), axis=1),...  74.5 us
    all_gather x1, waiting for transfers between devices, body(): portion = lax.all_gather(normed_own, 'dp', axis=0, tiled=True)  59 us
  transfers between devices with their start and end apart: 2, of which 2 were waited for; matrix products, arithmetic and copies ran while one was open for 2% of the time, Pallas kernels for 0%

commit v1 on v0

v1 whole, which is shorter than its diff:
```python
import jax
import jax.numpy as jnp
from jax import lax
from jax.sharding import PartitionSpec as P

D = 8192
HALF = D // 2


discount = 0.99
expectile = 0.7
conservative = 0.5
reward_step = 0.5
epsilon = 1e-05
weight_limit = 8.0


def contract_rows(left_side, right_side):
    return lax.dot_general(
        left_side, right_side, (((1,), (1,)), ((), ())), preferred_element_type=jnp.float32
    )


def contract_tokens(left_side, right_side):
    return lax.dot_general(
        left_side, right_side, (((0,), (0,)), ((), ())), preferred_element_type=jnp.float32
    )


def merge_totals(tops, totals, taken):
    top = jnp.max(tops, axis=0)
    return top, jnp.sum(totals * jnp.exp(tops - top[None]), axis=0), jnp.sum(taken, axis=0)


def body(
    hidden_state,
    norm_gain,
    critic_weight,
    policy_weight,
    value_weight,
    actions,
    rewards,
    done_flags,
    pad_mask,
):
    dp_size = lax.axis_size("dp")
    mp_size = lax.axis_size("mp")
    chip_count = mp_size // 2
    dp_index = lax.axis_index("dp")
    mp_index = lax.axis_index("mp")
    core = mp_index % 2
    core_swap = [(i, i ^ 1) for i in range(mp_size)]
    chip_groups = [[c + 2 * k for k in range(chip_count)] for c in range(2)]
    block_rows = hidden_state.shape[0]
    tokens = block_rows * dp_size

    def swap(array):
        return lax.ppermute(array, "mp", core_swap)

    def spread(array, axis, size, groups=None):
        copies = jnp.broadcast_to(array[None], (size,) + array.shape)
        return lax.all_to_all(copies, axis, 0, 0, axis_index_groups=groups)

    def half_rows(array, which):
        return lax.dynamic_slice_in_dim(array, which * HALF, HALF, 0)

    state_float = hidden_state.astype(jnp.float32)
    row_inverse = lax.rsqrt(jnp.mean(state_float * state_float, axis=1) + epsilon)
    unit_state = state_float * row_inverse[:, None]
    gain_float = norm_gain.astype(jnp.float32)
    normed_own = (unit_state * gain_float[None, :]).astype(jnp.bfloat16)

    with jax.named_scope("gather"):
        normed_half = lax.dynamic_slice_in_dim(normed_own, core * HALF, HALF, 1)
        mine = spread(normed_half, "dp", dp_size).reshape(tokens, HALF)
        other = swap(mine)

    with jax.named_scope("logits"):
        value_float = value_weight
        critic_mine, critic_other = half_rows(critic_weight, core), half_rows(critic_weight, 1 - core)
        policy_mine, policy_other = half_rows(policy_weight, core), half_rows(policy_weight, 1 - core)
        value_mine, value_other = half_rows(value_float, core), half_rows(value_float, 1 - core)

        def project(weight_mine, weight_other):
            return jnp.dot(mine, weight_mine, preferred_element_type=jnp.float32) + jnp.dot(
                other, weight_other, preferred_element_type=jnp.float32
            )

        critic_logits = project(critic_mine, critic_other)
        policy_logits = project(policy_mine, policy_other)
        values = project(value_mine, value_other)

    vocab_width = critic_weight.shape[1]
    block_index = dp_index * mp_size + mp_index
    columns = block_index * vocab_width + jnp.arange(vocab_width, dtype=jnp.int32)
    chosen = (actions[:, None] == columns[None, :]).astype(jnp.float32)

    with jax.named_scope("totals"):
        tops = jnp.stack([jnp.max(critic_logits, axis=1), jnp.max(policy_logits, axis=1)])
        totals = jnp.stack(
            [
                jnp.sum(jnp.exp(critic_logits - tops[0][:, None]), axis=1),
                jnp.sum(jnp.exp(policy_logits - tops[1][:, None]), axis=1),
            ]
        )
        taken = jnp.sum(critic_logits * chosen, axis=1)
        packed = jnp.concatenate([tops, totals, taken[None]], axis=0)

        def merge(parts):
            top, total, take = merge_totals(parts[:, 0:2], parts[:, 2:4], parts[:, 4])
            return jnp.concatenate([top, total, take[None]], axis=0)

        packed = merge(jnp.stack([packed, swap(packed)]))
        packed = merge(spread(packed, "mp", chip_count, chip_groups))
        packed = merge(spread(packed, "dp", dp_size))
        critic_max, policy_max, critic_total, policy_total, critic_taken = packed

    critic_probs = jnp.exp(critic_logits - critic_max[:, None]) / critic_total[:, None]
    policy_probs = jnp.exp(policy_logits - policy_max[:, None]) / policy_total[:, None]
    next_values = jnp.concatenate([values[1:], jnp.zeros((1,), jnp.float32)])
    target = (
        reward_step * rewards.astype(jnp.float32)
        + discount * (1.0 - done_flags.astype(jnp.float32)) * next_values
    )
    live_mask = pad_mask.astype(jnp.float32)
    advantage = critic_taken - values
    weights = jnp.where(advantage >= 0.0, expectile, 1.0 - expectile)
    value_coef = live_mask * -2.0 * weights * advantage
    critic_coef = live_mask * (2.0 * (critic_taken - target) - conservative)
    critic_grad = (
        conservative * live_mask[:, None] * critic_probs + critic_coef[:, None] * chosen
    ).astype(jnp.bfloat16)
    policy_grad = (live_mask[:, None] * (policy_probs - chosen)).astype(jnp.bfloat16)

    bound = 2.5 + jnp.abs(critic_coef)
    send_scale = (4.0 * 8192.0 / weight_limit) / bound
    back_scale = bound * (weight_limit / (4.0 * 8192.0))

    with jax.named_scope("reduce"):
        part_other = contract_rows(critic_grad, critic_other) + contract_rows(
            policy_grad, policy_other
        )
        arrived = swap((part_other * send_scale[:, None]).astype(jnp.float16))
        part_mine = contract_rows(critic_grad, critic_mine) + contract_rows(
            policy_grad, policy_mine
        )
        chip_part = (
            part_mine * send_scale[:, None] + arrived.astype(jnp.float32)
        ).astype(jnp.float16)
        chip_part = lax.all_to_all(chip_part.reshape(dp_size, block_rows, HALF), "dp", 0, 0)
        block_back = lax.dynamic_slice_in_dim(back_scale, dp_index * block_rows, block_rows, 0)
        block_coef = lax.dynamic_slice_in_dim(value_coef, dp_index * block_rows, block_rows, 0)
        block_part = jnp.sum(chip_part.astype(jnp.float32), axis=0) * block_back[:, None]
        unit_half = lax.dynamic_slice_in_dim(unit_state, core * HALF, HALF, 1)
        gain_part = jnp.sum(block_part * unit_half, axis=0)
        rows_out = jnp.concatenate(
            [
                block_part.reshape(chip_count, 2, HALF),
                jnp.broadcast_to(gain_part[None, None], (chip_count, 1, HALF)),
            ],
            axis=1,
        )
        rows_in = jnp.sum(
            lax.all_to_all(rows_out, "mp", 0, 0, axis_index_groups=chip_groups), axis=0
        )

    with jax.named_scope("gain"):
        value_half = value_mine.astype(jnp.float32)
        gain_block = rows_in[2] + value_half * jnp.sum(block_coef[:, None] * unit_half, axis=0)
        gain_mine = jnp.sum(spread(gain_block, "dp", dp_size), axis=0)
        gain_other = swap(gain_mine)
        first_core = core == 0
        grad_gain = jnp.concatenate(
            [
                jnp.where(first_core, gain_mine, gain_other),
                jnp.where(first_core, gain_other, gain_mine),
            ]
        )

    with jax.named_scope("hidden"):
        own_half = jnp.where(first_core, rows_in[0], rows_in[1])
        far_half = swap(jnp.where(first_core, rows_in[1], rows_in[0]))
        own_row = jnp.concatenate(
            [jnp.where(first_core, own_half, far_half), jnp.where(first_core, far_half, own_half)]
        )[None]
        own_coef = lax.dynamic_slice_in_dim(value_coef, block_index, 1, 0)
        own_unit = lax.dynamic_slice_in_dim(unit_state, mp_index, 1, 0)
        own_inverse = lax.dynamic_slice_in_dim(row_inverse, mp_index, 1, 0)
        normed_grad = own_row + own_coef[:, None] * value_weight.astype(jnp.float32)[None, :]
        scaled = normed_grad * gain_float[None, :]
        row_dot = jnp.sum(scaled * own_unit, axis=1)
        grad_hidden = (own_inverse[:, None] * (scaled - own_unit * row_dot[:, None] / D)).astype(
            jnp.bfloat16
        )

    with jax.named_scope("weights"):
        normed = jnp.concatenate(
            [jnp.where(first_core, mine, other), jnp.where(first_core, other, mine)], axis=1
        )
        grad_critic = contract_tokens(normed, critic_grad).astype(jnp.bfloat16)
        grad_value = jnp.sum(value_coef[:, None] * normed.astype(jnp.float32), axis=0)
    return (grad_hidden, grad_gain, grad_critic, grad_value)


def solution(mesh):
    placed = (
        P("dp", None),
        P(),
        P(None, ("dp", "mp")),
        P(None, ("dp", "mp")),
        P(),
        P(),
        P(),
        P(),
        P(),
    )
    return jax.shard_map(
        body,
        mesh=mesh,
        in_specs=placed,
        out_specs=(P(("dp", "mp"), None), P(), P(None, ("dp", "mp")), P()),
        check_vma=False,
    )
```

time: 602 us -> 179 us (0.30)
  waiting for transfers between devices: 322 us -> 55.3 us
  blocking collectives: 228 us -> 33.9 us
  starting transfers between devices: 0.08 us -> 37.5 us
  between operations: 14.2 us -> 0.98 us
  other arithmetic: 8.96 us -> 18.4 us
    unnamed x3 -> x0, waiting for transfers between devices: 263 us -> none
    psum x2 -> x0, blocking collectives: 152 us -> none  [the longest x1 77.6 us: body(): grad_gain = lax.psum(jnp.sum(normed_grad * own_unit, axis=0), ('dp', 'mp'))]
    pmax x1 -> x0, blocking collectives: 75.9 us -> none  [body(): critic_max, policy_max = lax.pmax((critic_top, policy_top), ('dp', 'mp'))]
    all_gather x1 -> x0, waiting for transfers between devices: 59 us -> none  [body(): portion = lax.all_gather(normed_own, 'dp', axis=0, tiled=True)]
    all_to_all x0 -> x5, waiting for transfers between devices: none -> 51.2 us  [the longest x1 28.3 us: body(): lax.all_to_all(chip_part.reshape(dp_size, block_rows, HALF), 'dp', 0, 0)]
    all_to_all x0 -> x1, blocking collectives: none -> 33.9 us  [spread(): return lax.all_to_all(copies, axis, 0, 0, axis_index_groups=groups)]
    all_to_all x0 -> x5, starting transfers between devices: none -> 26.9 us  [the longest x3 18.4 us: spread(): return lax.all_to_all(copies, axis, 0, 0, axis_index_groups=groups)]
    ppermute x0 -> x5, starting transfers between devices: none -> 10.6 us  [swap(): return lax.ppermute(array, 'mp', core_swap)]
  transfers between devices with their start and end apart: 2 -> 10, of which waited for: 2 -> 7; matrix products, arithmetic and copies ran while one was open for 2% -> 12% of each run, Pallas kernels for 0% -> 0%
where the time goes in v1:
time: 179 us; the launch traced here: 178 us
  waiting for transfers between devices  55.3 us (31%)
  starting transfers between devices  37.5 us (21%)
  blocking collectives  33.9 us (19%)
  matrix products  25.5 us (14%)
  other arithmetic  18.4 us (10%)
  local copies, waits for them, and re-layouts  6.48 us (4%)
    all_to_all x1, blocking collectives, spread(): return lax.all_to_all(copies, axis, 0, 0, axis_index_groups=groups)  33.9 us
    all_to_all x1, waiting for transfers between devices, body(): lax.all_to_all(chip_part.reshape(dp_size, block_rows, HALF), 'dp', 0, 0)  28.3 us
    all_to_all x3, starting transfers between devices, spread(): return lax.all_to_all(copies, axis, 0, 0, axis_index_groups=groups)  18.4 us
    all_to_all x1, waiting for transfers between devices, body(): lax.all_to_all(rows_out, 'mp', 0, 0, axis_index_groups=chip_groups)  12 us
    all_to_all x3, waiting for transfers between devices, spread(): return lax.all_to_all(copies, axis, 0, 0, axis_index_groups=groups)  11 us
    ppermute x5, starting transfers between devices, swap(): return lax.ppermute(array, 'mp', core_swap)  10.6 us
    dot_general x4, matrix products, contract_rows(): lax.dot_general(left_side, right_side, (((1,), (1,)), ((), ())), preferre...  8.02 us
    dot_general x3, matrix products, project(): jnp.dot(other, weight_other, preferred_element_type=jnp.float32)  7.42 us
  transfers between devices with their start and end apart: 10, of which 7 were waited for; matrix products, arithmetic and copies ran while one was open for 12% of the time, Pallas kernels for 0%

profile of v1, /device:TPU:1, one launch (start us, length us, event | category | flops | bytes accessed | tf_op | source)
XLA Modules:
  0.0 178.1 jit_solution(15317349587001089405)
XLA Ops:
  0.6 1.1 fusion.23
  1.8 1.1 convert_multiply_fusion
  2.9 0.7 dynamic-slice
  3.6 0.2 broadcast_in_dim.22
  3.8 33.9 %all_to_all.31 = bf16[16,16,4096]{2,1,0:T(8,128)(2,1)S(1)} all-to-all(bf16[16,16,4096]{2,1,0:T(8,128)(2,1)S(1)} %broadcast_in_dim.22), channel_id=1, replica_groups=mesh['dp'=16,'mp'=16] {'dp'}, dimensions={0} | all-to-all | bytes 4194304 | tf_op jit(solution)/shard_map/gather/all_to_all | solution.py:62
  37.7 2.7 %collective-permute-start = (bf16[256,4096]{1,0:T(8,128)(2,1)S(1)}, bf16[256,4096]{1,0:T(8,128)(2,1)}, u32[]{:S(2)}, u32[]{:S(2)}) collective-permute-start(bf16[256,4096]{1,0:T(8,128)(2,1)S(1)} %bitcast.32), channel_id=1, source_target_pairs={{0,1},{1,0},{2,3},{3,2},{4,5},{5,4},{6,7},{7,6},{8,9},{9,8},{10,11... | collective-permute-start | bytes 6291464 | tf_op jit(solution)/shard_map/gather/ppermute | solution.py:58
  40.4 2.7 %fusion.7 = f32[256,256]{0,1:T(8,128)S(1)} fusion(bf16[256,4096]{1,0:T(8,128)(2,1)S(1)} %bitcast.33, bf16[8192,256]{1,0:T(8,128)(2,1)} %param.12, s32[]{:T(128)S(6)} %select_n.86), kind=kOutput, calls=%fused_computation.16 | convolution fusion | flops 536870912 | bytes 4456452 | tf_op jit(solution)/shard_map/logits/dot_general | solution.py:85
  43.1 0.1 copy-done
  43.2 1.0 fusion.15
  44.2 0.1 collective-permute-done
  44.3 1.1 copy-done.2
  45.4 2.6 %fusion.66 = (f32[256]{0:T(256)S(1)}, f32[256,256]{0,1:T(8,128)S(1)}) fusion(f32[256,256]{0,1:T(8,128)S(1)} %fusion.7, bf16[256,4096]{1,0:T(8,128)(2,1)} %collective-permute-done, bf16[8192,256]{1,0:T(8,128)(2,1)S(1)} %copy-done.2, s32[]{:T(128)S(6)} %select_n.87), kind=kOutput, calls=%fused_computation.108 | convolution fusion | flops 537001728 | bytes 4719620 | tf_op jit(solution)/shard_map/logits/dot_general | solution.py:85
  48.0 0.1 exponential_reduce_fusion
  48.1 0.0 copy-start.8
  48.1 2.6 %fusion.65 = (f32[256]{0:T(256)S(1)}, f32[256,256]{0,1:T(8,128)S(1)}) fusion(f32[256,256]{0,1:T(8,128)S(1)} %fusion.15, bf16[256,4096]{1,0:T(8,128)(2,1)} %collective-permute-done, bf16[8192,256]{1,0:T(8,128)(2,1)S(1)} %copy-done, s32[]{:T(128)S(6)} %select_n.87), kind=kOutput, calls=%fused_computation.107 | convolution fusion | flops 537001728 | bytes 4719620 | tf_op jit(solution)/shard_map/logits/dot_general | solution.py:85
  50.7 0.1 fusion.24
  50.9 0.1 collective-permute-start.1
  51.1 1.1 collective-permute-done.1
  52.2 0.6 broadcast_in_dim.27
  52.9 8.2 %all-to-all-start.1 = ((f32[8,5,256]{2,1,0:T(8,128)}), f32[8,5,256]{2,1,0:T(8,128)S(1)}, u32[]{:S(2)}, u32[]{:S(2)}) async-start(f32[8,5,256]{2,1,0:T(8,128)} %broadcast_in_dim.27), calls=%async_computation.1 | async-start | bytes 131072 | tf_op jit(solution)/shard_map/totals/all_to_all | solution.py:62
  61.1 0.6 fusion.67
  61.7 6.5 %all-to-all-done.1 = f32[8,5,256]{2,1,0:T(8,128)S(1)} async-done(((f32[8,5,256]{2,1,0:T(8,128)}), f32[8,5,256]{2,1,0:T(8,128)S(1)}, u32[]{:S(2)}, u32[]{:S(2)}) %all-to-all-start.1) | async-done | bytes 40992 | tf_op jit(solution)/shard_map/totals/all_to_all | solution.py:62
  68.3 0.7 broadcast_in_dim.29
  69.0 3.6 %all-to-all-start.2 = ((f32[16,5,256]{2,1,0:T(8,128)}), f32[16,5,256]{2,1,0:T(8,128)S(1)}, u32[]{:S(2)}, u32[]{:S(2)}) async-start(f32[16,5,256]{2,1,0:T(8,128)} %broadcast_in_dim.29), calls=%async_computation.2 | async-start | bytes 262144 | tf_op jit(solution)/shard_map/totals/all_to_all | solution.py:62
  72.6 2.2 %fusion.68 = f32[1,256]{1,0:T(1,128)S(1)} fusion(bf16[256,4096]{1,0:T(8,128)(2,1)} %collective-permute-done, bf16[4096,1]{0,1:T(2,128)(2,1)S(1)} %reshape.83), kind=kOutput, calls=%fused_computation.110 | convolution fusion | flops 2097152 | bytes 2106368 | tf_op jit(solution)/shard_map/logits/dot_general | solution.py:85
  74.8 4.5 %all-to-all-done.2 = f32[16,5,256]{2,1,0:T(8,128)S(1)} async-done(((f32[16,5,256]{2,1,0:T(8,128)}), f32[16,5,256]{2,1,0:T(8,128)S(1)}, u32[]{:S(2)}, u32[]{:S(2)}) %all-to-all-start.2) | async-done | bytes 81952 | tf_op jit(solution)/shard_map/totals/all_to_all | solution.py:62
  79.4 0.1 slice.50
  79.4 0.1 fusion.51
  79.6 0.1 fusion.30
  79.6 2.6 %fusion.9 = f32[256,4096]{1,0:T(8,128)S(1)} fusion(bf16[8192,256]{1,0:T(8,128)(2,1)} %param.11, s32[]{:T(128)S(6)} %select_n.87, f32[256,256]{0,1:T(8,128)S(1)} %get-tuple-element.31, f32[256]{0:T(256)S(1)} %get-tuple-element.9, f32[256]{0:T(256)S(1)} %bitcast.45, f32[256]{0:T(256)S(1)} %bitcast.42, s32[256]{0:T(256)S(1)} %copy-done.7, ...), kind=kOutput, calls=%fused_computation.18 | convolution fusion | flops 537329664 | bytes 6559748 | tf_op jit(solution)/shard_map/reduce/dot_general | solution.py:19
  82.2 0.2 copy-done.3
  82.5 1.5 fusion.2
  83.9 3.3 %collective-permute-start.2 = (f16[256,4096]{1,0:T(8,128)(2,1)S(1)}, f16[256,4096]{1,0:T(8,128)(2,1)S(1)}, u32[]{:S(2)}, u32[]{:S(2)}) collective-permute-start(f16[256,4096]{1,0:T(8,128)(2,1)S(1)} %fusion.2), channel_id=1, source_target_pairs={{0,1},{1,0},{2,3},{3,2},{4,5},{5,4},{6,7},{7,6},{8,9},{9,8},{10,11... | collective-permute-start | bytes 6291464 | tf_op jit(solution)/shard_map/reduce/ppermute | solution.py:58
  87.2 0.8 fusion.13
  88.1 2.9 %collective-permute-done.2 = f16[256,4096]{1,0:T(8,128)(2,1)S(1)} collective-permute-done((f16[256,4096]{1,0:T(8,128)(2,1)S(1)}, f16[256,4096]{1,0:T(8,128)(2,1)S(1)}, u32[]{:S(2)}, u32[]{:S(2)}) %collective-permute-start.2) | collective-permute-done | bytes 2097184 | tf_op jit(solution)/shard_map/reduce/ppermute | solution.py:58
  91.0 3.1 %add_convert_fusion = f16[256,4096]{1,0:T(8,128)(2,1)} fusion(f16[256,4096]{1,0:T(8,128)(2,1)S(1)} %collective-permute-done.2, f32[256]{0:T(256)S(1)} %fusion.52, f32[256,4096]{1,0:T(8,128)S(1)} %fusion.13, bf16[8192,256]{1,0:T(8,128)(2,1)S(1)} %copy-done.3, s32[]{:T(128)S(6)} %select_n.86, f32[256,256]{0,1:T(8,128)S(1)} %get-tuple-element.33, ...), kind=kOutput, calls=%fused_computation.9 | convolution fusion | flops 542572544 | bytes 10754052 | tf_op jit(solution)/shard_map/reduce/dot_general | solution.py:19
  94.1 4.4 %all-to-all-start.3 = ((f16[16,16,4096]{2,1,0:T(8,128)(2,1)}), f16[16,16,4096]{2,1,0:T(8,128)(2,1)}, u32[]{:S(2)}, u32[]{:S(2)}) async-start(f16[16,16,4096]{2,1,0:T(8,128)(2,1)} %bitcast.36), calls=%async_computation.3 | async-start | bytes 4194304 | tf_op jit(solution)/shard_map/reduce/all_to_all | solution.py:150
  98.6 0.7 dynamic_slice.39
  99.3 0.1 dynamic_slice.51
  99.3 0.1 dynamic_slice.47
  99.4 0.1 mul.245
  99.5 28.3 %all-to-all-done.3 = f16[16,16,4096]{2,1,0:T(8,128)(2,1)} async-done(((f16[16,16,4096]{2,1,0:T(8,128)(2,1)}), f16[16,16,4096]{2,1,0:T(8,128)(2,1)}, u32[]{:S(2)}, u32[]{:S(2)}) %all-to-all-start.3) | async-done | bytes 2097184 | tf_op jit(solution)/shard_map/reduce/all_to_all | solution.py:150
  127.8 1.9 %convert_reduce_fusion = f32[16,4096]{1,0:T(8,128)S(1)} fusion(f16[16,16,4096]{2,1,0:T(8,128)(2,1)} %all-to-all-done.3), kind=kLoop, calls=%fused_computation.8 | loop fusion | flops 2031616 | bytes 2359296 | tf_op jit(solution)/shard_map/reduce/reduce_sum | solution.py:153
  129.7 0.2 reduce_sum.166
  129.8 0.2 multiply_reduce_fusion.1
  130.0 0.2 broadcast_multiply_fusion
  130.2 0.1 broadcast_in_dim.30
  130.3 1.0 pad_maximum_fusion.2
  131.3 4.1 %all-to-all-start.4 = ((f32[8,3,4096]{2,1,0:T(4,128)}), f32[8,3,4096]{2,1,0:T(4,128)}, u32[]{:S(2)}, u32[]{:S(2)}) async-start(f32[8,3,4096]{2,1,0:T(4,128)} %pad_maximum_fusion.2), calls=%async_computation.4 | async-start | bytes 1048576 | tf_op jit(solution)/shard_map/reduce/all_to_all | solution.py:164
  135.4 3.9 %broadcast_select_fusion.1 = (bf16[256,4096]{1,0:T(8,128)(2,1)}, bf16[256,4096]{1,0:T(8,128)(2,1)}) fusion(bf16[256,4096]{1,0:T(8,128)(2,1)} %collective-permute-done, pred[]{:T(512)S(6)} %eq.18, bf16[16,16,4096]{2,1,0:T(8,128)(2,1)S(1)} %all_to_all.31), kind=kLoop, calls=%fused_computation.11 | loop fusion | flops 2097152 | bytes 8388609 | tf_op jit(solution)/shard_map/weights/jit(_where)/select_n | solution.py:198
  139.4 12.0 %all-to-all-done.4 = f32[8,3,4096]{2,1,0:T(4,128)} async-done(((f32[8,3,4096]{2,1,0:T(4,128)}), f32[8,3,4096]{2,1,0:T(4,128)}, u32[]{:S(2)}, u32[]{:S(2)}) %all-to-all-start.4) | async-done | bytes 393248 | tf_op jit(solution)/shard_map/reduce/all_to_all | solution.py:164
  151.3 1.1 reduce_sum.168
  152.5 0.9 broadcast_in_dim.33
  153.4 6.6 %all-to-all-start.5 = ((f32[16,1,4096]{2,1,0:T(1,128)}), f32[16,1,4096]{2,1,0:T(1,128)S(1)}, u32[]{:S(2)}, u32[]{:S(2)}) async-start(f32[16,1,4096]{2,1,0:T(1,128)} %broadcast_in_dim.33), calls=%async_computation.5 | async-start | bytes 524288 | tf_op jit(solution)/shard_map/gain/all_to_all | solution.py:62
  160.0 5.8 %convolution_convert_fusion = bf16[8192,256]{1,0:T(8,128)(2,1)} fusion(bf16[256,4096]{1,0:T(8,128)(2,1)} %get-tuple-element.15, bf16[256,4096]{1,0:T(8,128)(2,1)} %get-tuple-element.14, f32[256,256]{0,1:T(8,128)S(1)} %get-tuple-element.31, f32[256]{0:T(256)S(1)} %get-tuple-element.9, f32[256]{0:T(256)S(1)} %bitcast.47, f32[256]{0:T(256)S(1)} %bitcast.44, ...), kind=kOutput, calls=%fused_computation | convolution fusion | flops 1084686336 | bytes 8656896 | tf_op jit(solution)/shard_map/weights/dot_general | solution.py:25
  165.8 1.7 collective-permute-start.3
  167.5 0.2 reduce_sum.171
  167.7 2.8 %collective-permute-start.4 = (f32[4096]{0:T(1024)S(1)}, f32[4096]{0:T(1024)S(1)}, u32[]{:S(2)}, u32[]{:S(2)}) collective-permute-start(f32[4096]{0:T(1024)S(1)} %reduce_sum.171), channel_id=1, source_target_pairs={{0,1},{1,0},{2,3},{3,2},{4,5},{5,4},{6,7},{7,6},{8,9},{9,8},{10,11... | collective-permute-start | bytes 49160 | tf_op jit(solution)/shard_map/gain/ppermute | solution.py:58
  170.5 2.9 %multiply_reduce_fusion = f32[8192]{0:T(1024)} fusion(f32[256]{0:T(256)S(1)} %get-tuple-element.10, bf16[256,4096]{1,0:T(8,128)(2,1)} %get-tuple-element.15, bf16[256,4096]{1,0:T(8,128)(2,1)S(1)} %copy-done.4), kind=kLoop, calls=%fused_computation.1 | loop fusion | flops 12574720 | bytes 4228096 | tf_op jit(solution)/shard_map/weights/reduce_sum | solution.py:201
  173.4 0.6 dynamic_slice.49
  174.0 0.7 fusion.31
  174.7 0.8 multiply_reduce_fusion.3
  175.4 0.6 pad_maximum_fusion.3
  176.1 2.1 %multiply_convert_fusion.1 = bf16[1,8192]{1,0:T(2,128)(2,1)} fusion(f32[1,8192]{1,0:T(1,128)S(1)} %bitcast.38, f32[16,8192]{1,0:T(8,128)S(1)} %convert_multiply_fusion, s32[]{:T(128)S(6)} %select_n.82, f32[]{:T(128)} %multiply_reduce_fusion.3, f32[]{:T(128)} %bitcast), kind=kLoop, calls=%fused_computation.52 | loop fusion | flops 40960 | bytes 81932 | tf_op jit(solution)/shard_map/hidden/convert_element_type | solution.py:192
  (48 shorter events, 0.5 us)
Async XLA Ops:
  37.7 6.6 %collective-permute-start = (bf16[256,4096]{1,0:T(8,128)(2,1)S(1)}, bf16[256,4096]{1,0:T(8,128)(2,1)}, u32[]{:S(2)}, u32[]{:S(2)}) collective-permute-start(bf16[256,4096]{1,0:T(8,128)(2,1)S(1)} %bitcast.32), channel_id=1, source_target_pairs={{0,1},{1,0},{2,3},{3,2},{4,5},{5,4},{6,7},{7,6},{8,9},{9,8},{10,11... | collective-permute-start | bytes 6291464 | tf_op jit(solution)/shard_map/gather/ppermute | solution.py:58
  40.4 2.8 %copy-start = (bf16[8192,256]{1,0:T(8,128)(2,1)S(1)}, bf16[8192,256]{1,0:T(8,128)(2,1)}, u32[]{:S(2)}) copy-start(bf16[8192,256]{1,0:T(8,128)(2,1)} %param.11) | copy-start | bytes 12582916
  43.2 2.2 %copy-start.2 = (bf16[8192,256]{1,0:T(8,128)(2,1)S(1)}, bf16[8192,256]{1,0:T(8,128)(2,1)}, u32[]{:S(2)}) copy-start(bf16[8192,256]{1,0:T(8,128)(2,1)} %param.12) | copy-start | bytes 12582916
  48.1 2.6 %copy-start.7 = (s32[256]{0:T(256)S(1)}, s32[256]{0:T(256)}, u32[]{:S(2)}) copy-start(s32[256]{0:T(256)} %param.14) | copy-start | bytes 3076
  48.1 2.9 %copy-start.6 = (bf16[8192]{0:T(1024)(128)(2,1)S(1)}, bf16[8192]{0:T(1024)(128)(2,1)}, u32[]{:S(2)}) copy-start(bf16[8192]{0:T(1024)(128)(2,1)} %param.13) | copy-start | bytes 49156
  48.1 2.9 %copy-start.8 = (s32[256]{0:T(256)S(1)}, s32[256]{0:T(256)}, u32[]{:S(2)}) copy-start(s32[256]{0:T(256)} %param.17) | copy-start | bytes 3076
  50.9 1.3 collective-permute-start.1
  52.9 15.3 %all-to-all-start.1 = ((f32[8,5,256]{2,1,0:T(8,128)}), f32[8,5,256]{2,1,0:T(8,128)S(1)}, u32[]{:S(2)}, u32[]{:S(2)}) async-start(f32[8,5,256]{2,1,0:T(8,128)} %broadcast_in_dim.27), calls=%async_computation.1 | async-start | bytes 131072 | tf_op jit(solution)/shard_map/totals/all_to_all | solution.py:62
  61.1 18.4 %copy-start.9 = (s32[256]{0:T(256)S(1)}, s32[256]{0:T(256)}, u32[]{:S(2)}) copy-start(s32[256]{0:T(256)} %param.16) | copy-start | bytes 3076
  61.1 18.4 %copy-start.10 = (s32[256]{0:T(256)S(1)}, s32[256]{0:T(256)}, u32[]{:S(2)}) copy-start(s32[256]{0:T(256)} %param.15) | copy-start | bytes 3076
  69.0 10.3 %all-to-all-start.2 = ((f32[16,5,256]{2,1,0:T(8,128)}), f32[16,5,256]{2,1,0:T(8,128)S(1)}, u32[]{:S(2)}, u32[]{:S(2)}) async-start(f32[16,5,256]{2,1,0:T(8,128)} %broadcast_in_dim.29), calls=%async_computation.2 | async-start | bytes 262144 | tf_op jit(solution)/shard_map/totals/all_to_all | solution.py:62
  79.6 2.8 %copy-start.3 = (bf16[8192,256]{1,0:T(8,128)(2,1)S(1)}, bf16[8192,256]{1,0:T(8,128)(2,1)}, u32[]{:S(2)}) copy-start(bf16[8192,256]{1,0:T(8,128)(2,1)} %param.12) | copy-start | bytes 12582916
  82.5 4.8 %copy-start.1 = (bf16[8192,256]{1,0:T(8,128)(2,1)S(1)}, bf16[8192,256]{1,0:T(8,128)(2,1)}, u32[]{:S(2)}) copy-start(bf16[8192,256]{1,0:T(8,128)(2,1)} %param.11) | copy-start | bytes 12582916
  83.9 7.1 %collective-permute-start.2 = (f16[256,4096]{1,0:T(8,128)(2,1)S(1)}, f16[256,4096]{1,0:T(8,128)(2,1)S(1)}, u32[]{:S(2)}, u32[]{:S(2)}) collective-permute-start(f16[256,4096]{1,0:T(8,128)(2,1)S(1)} %fusion.2), channel_id=1, source_target_pairs={{0,1},{1,0},{2,3},{3,2},{4,5},{5,4},{6,7},{7,6},{8,9},{9,8},{10,11... | collective-permute-start | bytes 6291464 | tf_op jit(solution)/shard_map/reduce/ppermute | solution.py:58
  94.1 33.6 %all-to-all-start.3 = ((f16[16,16,4096]{2,1,0:T(8,128)(2,1)}), f16[16,16,4096]{2,1,0:T(8,128)(2,1)}, u32[]{:S(2)}, u32[]{:S(2)}) async-start(f16[16,16,4096]{2,1,0:T(8,128)(2,1)} %bitcast.36), calls=%async_computation.3 | async-start | bytes 4194304 | tf_op jit(solution)/shard_map/reduce/all_to_all | solution.py:150
  131.3 20.0 %all-to-all-start.4 = ((f32[8,3,4096]{2,1,0:T(4,128)}), f32[8,3,4096]{2,1,0:T(4,128)}, u32[]{:S(2)}, u32[]{:S(2)}) async-start(f32[8,3,4096]{2,1,0:T(4,128)} %pad_maximum_fusion.2), calls=%async_computation.4 | async-start | bytes 1048576 | tf_op jit(solution)/shard_map/reduce/all_to_all | solution.py:164
  153.4 14.1 %all-to-all-start.5 = ((f32[16,1,4096]{2,1,0:T(1,128)}), f32[16,1,4096]{2,1,0:T(1,128)S(1)}, u32[]{:S(2)}, u32[]{:S(2)}) async-start(f32[16,1,4096]{2,1,0:T(1,128)} %broadcast_in_dim.33), calls=%async_computation.5 | async-start | bytes 524288 | tf_op jit(solution)/shard_map/gain/all_to_all | solution.py:62
  160.0 10.5 %copy-start.4 = (bf16[256,4096]{1,0:T(8,128)(2,1)S(1)}, bf16[256,4096]{1,0:T(8,128)(2,1)}, u32[]{:S(2)}) copy-start(bf16[256,4096]{1,0:T(8,128)(2,1)} %get-tuple-element.14) | copy-start | bytes 6291460
  165.8 8.2 %collective-permute-start.3 = (f32[4096]{0:T(1024)S(1)}, f32[4096]{0:T(1024)S(1)}, u32[]{:S(2)}, u32[]{:S(2)}) collective-permute-start(f32[4096]{0:T(1024)S(1)} %bitcast.48), channel_id=1, source_target_pairs={{0,1},{1,0},{2,3},{3,2},{4,5},{5,4},{6,7},{7,6},{8,9},{9,8},{10,11... | collective-permute-start | bytes 49160 | tf_op jit(solution)/shard_map/hidden/ppermute | solution.py:58
  167.7 6.3 %copy-start.5 = (bf16[8192]{0:T(1024)(128)(2,1)S(1)}, bf16[8192]{0:T(1024)(128)(2,1)}, u32[]{:S(2)}) copy-start(bf16[8192]{0:T(1024)(128)(2,1)} %param.10) | copy-start | bytes 49156
  167.7 6.3 %collective-permute-start.4 = (f32[4096]{0:T(1024)S(1)}, f32[4096]{0:T(1024)S(1)}, u32[]{:S(2)}, u32[]{:S(2)}) collective-permute-start(f32[4096]{0:T(1024)S(1)} %reduce_sum.171), channel_id=1, source_target_pairs={{0,1},{1,0},{2,3},{3,2},{4,5},{5,4},{6,7},{7,6},{8,9},{9,8},{10,11... | collective-permute-start | bytes 49160 | tf_op jit(solution)/shard_map/gain/ppermute | solution.py:58

commit v2 on v0

v2 whole, which is shorter than its diff:
```python
import functools
import math

import jax
import jax.numpy as jnp
from jax import lax
from jax.experimental import pallas as pl
from jax.experimental.pallas import tpu as pltpu
from jax.sharding import PartitionSpec as P

D = 8192
HALF = D // 2
LANES = 128
TILES = HALF // LANES
CHUNK_TILES = 8
CHUNK = CHUNK_TILES * LANES
CHUNKS = TILES // CHUNK_TILES


discount = 0.99
expectile = 0.7
conservative = 0.5
reward_step = 0.5
epsilon = 1e-05
unit_limit = 91.0
half_limit = 32768.0

f32 = jnp.float32
bf16 = jnp.bfloat16
f16 = jnp.float16

roomy = pltpu.CompilerParams(vmem_limit_bytes=16 * 1024 * 1024)


def whole(shape):
    return pl.BlockSpec(shape, lambda *_: (0,) * len(shape))


def to_columns(rows):
    tokens = rows.shape[1]
    filled = jnp.concatenate([rows, jnp.zeros((LANES - rows.shape[0], tokens), f32)], axis=0)
    return jnp.transpose(filled)


def lane_pack(columns):
    tokens = columns[0].shape[0]
    lane = lax.broadcasted_iota(jnp.int32, (tokens, LANES), 1)
    packed = jnp.zeros((tokens, LANES), f32)
    for k, column in enumerate(columns):
        packed = jnp.where(lane == k, column, packed)
    return packed


def inverse_column(half, tile_ref):
    parts = gathered_tile(half, tile_ref, 0)
    return parts[:, 0:1] + parts[:, 1:2] + parts[:, 2:3]


def gathered_place(half, group, side):
    x, y = divmod(group, side)
    return jnp.where(half == 0, y * side + x, x * side + y)


def reduced_place(half, group, side):
    x, y = divmod(group, side)
    return jnp.where(half == 0, x * side + y, y * side + x)


def gathered_tile(half, state_ref, tile):
    groups = state_ref.shape[0]
    side = math.isqrt(groups)
    return jnp.concatenate(
        [
            state_ref[gathered_place(half, group, side), tile].astype(f32)
            for group in range(groups)
        ],
        axis=0,
    )


def normed_tile(half, state_ref, tile, inverse, gain_ref):
    gain = gain_ref[:, tile * LANES : (tile + 1) * LANES].astype(f32)
    unit = gathered_tile(half, state_ref, tile) * inverse
    return (unit * gain).astype(bf16)


def norm_kernel(core_ref, state_ref, half_ref, out_ref):
    state = state_ref[...].astype(f32)
    mean = jnp.sum(state * state, axis=1, keepdims=True) / D
    inverse = lax.rsqrt(mean + epsilon)
    high = inverse.astype(bf16).astype(f32)
    middle = (inverse - high).astype(bf16).astype(f32)
    low = inverse - high - middle
    packed = lane_pack([high, middle, low]).astype(bf16)
    copies = out_ref.shape[0]
    for copy in range(copies):
        for tile in range(TILES):
            out_ref[copy, tile] = half_ref[:, tile * LANES : (tile + 1) * LANES]
        out_ref[copy, TILES] = packed


def project_kernel(
    last,
    core_ref,
    block_ref,
    state_ref,
    inverse_ref,
    gain_ref,
    value_ref,
    critic_ref,
    policy_ref,
    *rest,
):
    if last:
        sums_in, value_in, top_in, action_ref, *rest = rest
        logits_ref, totals_ref, own_ref, value_acc, normed_ref = rest
    else:
        logits_ref, value_acc, normed_ref = rest
    step = pl.program_id(0)
    tokens = normed_ref.shape[0]
    half = core_ref[0]
    inverse = inverse_column(half, inverse_ref)
    value_part = jnp.zeros((tokens, LANES), f32)
    for tile in range(CHUNK_TILES):
        where = slice(tile * LANES, (tile + 1) * LANES)
        normed = normed_tile(half, state_ref, tile, inverse, gain_ref)
        normed_ref[:, where] = normed
        value_part = value_part + normed.astype(f32) * value_ref[:, where].astype(f32)
    left = normed_ref[...]
    width = critic_ref.shape[1]
    critic = jnp.dot(left, critic_ref[...], preferred_element_type=f32)
    policy = jnp.dot(left, policy_ref[...], preferred_element_type=f32)

    @pl.when(step == 0)
    def _():
        value_acc[...] = value_part
        if last:
            logits_ref[:, :width] = sums_in[:, :width] + critic
            logits_ref[:, width:] = sums_in[:, width:] + policy
        else:
            logits_ref[:, :width] = critic
            logits_ref[:, width:] = policy

    @pl.when(step > 0)
    def _():
        value_acc[...] += value_part
        logits_ref[:, :width] += critic
        logits_ref[:, width:] += policy

    if last:

        @pl.when(step == CHUNKS - 1)
        def _():
            critic_logits = logits_ref[:, :width]
            policy_logits = logits_ref[:, width:]
            critic_top = jnp.max(critic_logits, axis=1, keepdims=True)
            policy_top = jnp.max(policy_logits, axis=1, keepdims=True)
            critic_total = jnp.sum(jnp.exp(critic_logits - critic_top), axis=1, keepdims=True)
            policy_total = jnp.sum(jnp.exp(policy_logits - policy_top), axis=1, keepdims=True)
            column = lax.broadcasted_iota(jnp.int32, (tokens, width), 1) + block_ref[0] * width
            action = to_columns(action_ref[...])[:, 0:1].astype(jnp.int32)
            taken = jnp.sum(
                jnp.where(column == action, critic_logits, 0.0), axis=1, keepdims=True
            )
            value = jnp.sum(value_in[...], axis=1, keepdims=True) + jnp.sum(
                value_acc[...], axis=1, keepdims=True
            )
            weight_top = jnp.broadcast_to(
                jnp.max(top_in[...], axis=1, keepdims=True), (tokens, 1)
            )
            packed = jnp.transpose(
                lane_pack(
                    [
                        critic_top,
                        policy_top,
                        critic_total,
                        policy_total,
                        taken,
                        weight_top,
                        value,
                    ]
                )
            )[:8]
            own_ref[...] = packed
            for copy in range(totals_ref.shape[0]):
                totals_ref[copy] = packed


def largest_kernel(critic_ref, policy_ref, top_ref):
    width = critic_ref.shape[1]
    largest = jnp.maximum(jnp.abs(critic_ref[...]), jnp.abs(policy_ref[...]))
    largest = jnp.max(largest.reshape(-1, 16, width), axis=0).astype(f32)
    largest = jnp.max(largest, axis=0, keepdims=True)
    step = pl.program_id(0)

    @pl.when(step == 0)
    def _():
        top_ref[...] = largest

    @pl.when(step > 0)
    def _():
        top_ref[...] = jnp.maximum(top_ref[...], largest)


def merge_parts(parts):
    tops = parts[:, 0:2]
    top = jnp.max(tops, axis=0)
    total = jnp.sum(parts[:, 2:4] * jnp.exp(tops - top[None]), axis=0)
    taken = jnp.sum(parts[:, 4:5], axis=0)
    weight_top = jnp.max(parts[:, 5:6], axis=0)
    return top, total, taken, weight_top


def merge_kernel(parts_ref, out_ref):
    tokens = parts_ref.shape[2]
    packed = jnp.concatenate([*merge_parts(parts_ref[...]), jnp.zeros((2, tokens), f32)], axis=0)
    for copy in range(out_ref.shape[0]):
        out_ref[copy] = packed


def turn(left, right):
    return lax.dot_general(left, right, (((1,), (1,)), ((), ())), preferred_element_type=f32)


def part_kernel(with_grads, core_ref, block_ref, *refs):
    if with_grads:
        parts_ref, own_ref, info_ref, logits_ref, *refs = refs
        state_ref, inverse_ref, critic_ref, policy_ref, out_ref, grads_ref, column_ref, gain_acc = refs
    else:
        grads_ref, column_ref, *refs = refs
        state_ref, inverse_ref, critic_ref, policy_ref, out_ref, gain_acc = refs
    step = pl.program_id(0)
    tokens = grads_ref.shape[0]
    width = critic_ref.shape[1]
    groups, _, rows, _ = out_ref.shape

    if with_grads:

        @pl.when(step == 0)
        def _():
            top, total, critic_taken, weight_top = merge_parts(parts_ref[...])
            values = own_ref[6:7]
            action, reward, done, live = (info_ref[k : k + 1] for k in range(4))
            place = lax.broadcasted_iota(jnp.int32, (1, tokens), 1)
            next_values = jnp.where(place == tokens - 1, 0.0, pltpu.roll(values, tokens - 1, 1))
            target = reward_step * reward + discount * (1.0 - done) * next_values
            advantage = critic_taken - values
            weights = jnp.where(advantage >= 0.0, expectile, 1.0 - expectile)
            value_coef = live * -2.0 * weights * advantage
            critic_coef = live * (2.0 * (critic_taken - target) - conservative)
            bound = (2.5 + jnp.abs(critic_coef)) * jnp.maximum(weight_top, 1e-20)
            gain_bound = jnp.sum(bound, axis=1, keepdims=True) * unit_limit
            first = to_columns(
                jnp.concatenate(
                    [
                        value_coef,
                        half_limit / bound,
                        bound / half_limit,
                        jnp.broadcast_to(half_limit / gain_bound, (1, tokens)),
                        jnp.broadcast_to(gain_bound / half_limit, (1, tokens)),
                        critic_coef,
                        action,
                        live,
                    ],
                    axis=0,
                )
            )
            column_ref[...] = first
            second = to_columns(
                jnp.concatenate([top, total, jnp.zeros((4, tokens), f32)], axis=0)
            )
            coef = first[:, 5:6]
            live_column = first[:, 7:8]
            column = lax.broadcasted_iota(jnp.int32, (tokens, width), 1) + block_ref[0] * width
            chosen = (column == first[:, 6:7].astype(jnp.int32)).astype(f32)
            critic_probs = jnp.exp(logits_ref[:, :width] - second[:, 0:1]) / second[:, 2:3]
            policy_probs = jnp.exp(logits_ref[:, width:] - second[:, 1:2]) / second[:, 3:4]
            grads_ref[:, :width] = (
                conservative * live_column * critic_probs + coef * chosen
            ).astype(bf16)
            grads_ref[:, width:] = (live_column * (policy_probs - chosen)).astype(bf16)

    @pl.when(step < CHUNKS)
    def _():
        half = core_ref[0]
        side = math.isqrt(groups)
        inverse = inverse_column(half, inverse_ref)
        part = turn(grads_ref[:, :width], critic_ref[...]) + turn(
            grads_ref[:, width:], policy_ref[...]
        )
        scale = column_ref[:, 1:2]
        gains = []
        for tile in range(CHUNK_TILES):
            block = part[:, tile * LANES : (tile + 1) * LANES]
            scaled = block * scale
            for group in range(groups):
                out_ref[reduced_place(half, group, side), tile] = scaled[
                    group * rows : (group + 1) * rows
                ]
            unit = gathered_tile(half, state_ref, tile) * inverse
            gains.append(jnp.sum(block * unit, axis=0, keepdims=True))
        gain_acc[pl.ds(pl.multiple_of(step * CHUNK_TILES, CHUNK_TILES), CHUNK_TILES)] = (
            jnp.concatenate(gains, axis=0)
        )

    @pl.when(step == CHUNKS)
    def _():
        gain = (gain_acc[...] * column_ref[0:1, 3:4]).reshape(TILES // rows, rows, LANES)
        for group in range(groups):
            out_ref[group, : TILES // rows] = gain


def weights_kernel(
    core_ref,
    mine_ref,
    mine_inverse_ref,
    other_ref,
    other_inverse_ref,
    gain_ref,
    grads_ref,
    column_ref,
    critic_ref,
    value_ref,
    extra_ref,
    normed_ref,
):
    step = pl.program_id(0)
    coef = column_ref[:, 0:1]

    def write(half, state_ref, inverse):
        for tile in range(CHUNK_TILES):
            where = slice(tile * LANES, (tile + 1) * LANES)
            normed = normed_tile(half, state_ref, tile, inverse, gain_ref)
            normed_ref[:, where] = normed
            value_ref[:, where] = jnp.sum(normed.astype(f32) * coef, axis=0, keepdims=True)
        critic_ref[...] = lax.dot_general(
            normed_ref[...], grads_ref[...], (((0,), (0,)), ((), ())), preferred_element_type=f32
        ).astype(bf16)

    @pl.when(step < CHUNKS)
    def _():
        half = core_ref[0]
        inverse = inverse_column(half, mine_inverse_ref)
        write(half, mine_ref, inverse)
        weighted = inverse * coef
        extra_ref[...] = jnp.concatenate(
            [
                jnp.sum(gathered_tile(half, mine_ref, tile) * weighted, axis=0, keepdims=True)
                for tile in range(CHUNK_TILES)
            ],
            axis=0,
        )

    @pl.when(step >= CHUNKS)
    def _():
        half = 1 - core_ref[0]
        write(half, other_ref, inverse_column(half, other_inverse_ref))


def split_kernel(block_ref, out_ref):
    peers = out_ref.shape[0]
    rows = 2 * peers
    for peer in range(peers):
        for k in range(2):
            out_ref[peer, k * TILES : (k + 1) * TILES] = block_ref[
                pl.ds(2 * peer + k, TILES, stride=rows)
            ]
        out_ref[peer, 2 * TILES :] = block_ref[TILES * rows :]


def finish_kernel(
    core_ref,
    column_ref,
    own_ref,
    far_ref,
    own_extra_ref,
    far_extra_ref,
    state_ref,
    weight_ref,
    value_ref,
    hidden_ref,
    gain_ref,
):
    first = core_ref[0] == 0
    own_half = jnp.where(first, own_ref[:TILES], own_ref[TILES : 2 * TILES])
    far_half = jnp.where(first, far_ref[:TILES], far_ref[TILES : 2 * TILES])
    row = jnp.concatenate(
        [jnp.where(first, own_half, far_half), jnp.where(first, far_half, own_half)], axis=0
    )
    value_coef = column_ref[:, 0:1]
    row_back = column_ref[:, 2:3]
    gain_back = column_ref[:, 4:5]
    value = value_ref[...].astype(f32)
    own_gain = own_ref[2 * TILES :] * gain_back
    far_gain = far_ref[2 * TILES :] * gain_back
    own_extra = own_extra_ref[...]
    far_extra = far_extra_ref[...]
    gain_ref[:TILES] = (
        jnp.where(first, own_gain, far_gain)
        + jnp.where(first, own_extra, far_extra) * value[:TILES]
    )
    gain_ref[TILES:] = (
        jnp.where(first, far_gain, own_gain)
        + jnp.where(first, far_extra, own_extra) * value[TILES:]
    )
    state = state_ref[...].astype(f32)
    mean = jnp.sum(jnp.sum(state * state, axis=1, keepdims=True), axis=0, keepdims=True) / D
    inverse = lax.rsqrt(mean + epsilon)
    unit = state * inverse
    normed_grad = row * row_back + value_coef * value
    scaled = normed_grad * weight_ref[...].astype(f32)
    row_dot = jnp.sum(jnp.sum(scaled * unit, axis=1, keepdims=True), axis=0, keepdims=True)
    grad = inverse * (scaled - unit * row_dot / D)
    for tile in range(2 * TILES):
        hidden_ref[:, tile * LANES : (tile + 1) * LANES] = grad[tile : tile + 1].astype(bf16)


def contract_tokens(left_side, right_side):
    return lax.dot_general(
        left_side, right_side, (((0,), (0,)), ((), ())), preferred_element_type=f32
    )


def body(
    hidden_state,
    norm_gain,
    critic_weight,
    policy_weight,
    value_weight,
    actions,
    rewards,
    done_flags,
    pad_mask,
):
    dp_size = lax.axis_size("dp")
    mp_size = lax.axis_size("mp")
    chip_count = mp_size // 2
    dp_index = lax.axis_index("dp")
    mp_index = lax.axis_index("mp")
    core = mp_index % 2
    core_swap = [(i, i ^ 1) for i in range(mp_size)]
    chip_groups = [[c + 2 * k for k in range(chip_count)] for c in range(2)]
    rows = hidden_state.shape[0]
    tokens = rows * dp_size
    width = critic_weight.shape[1]
    block_index = dp_index * mp_size + mp_index
    core_scalar = core.astype(jnp.int32).reshape(1)
    far_scalar = 1 - core_scalar
    block_scalar = block_index.astype(jnp.int32).reshape(1)

    def swap(array):
        return lax.ppermute(array, "mp", core_swap)

    gain_row = norm_gain.reshape(1, D)
    value_row = value_weight.reshape(1, D)
    info = jnp.stack([actions, rewards, done_flags, pad_mask] + [pad_mask] * 4).astype(f32)

    side = math.isqrt(dp_size)

    def axis_groups(turned):
        groups = []
        for c in range(2):
            for z in range(chip_count):
                for line in range(side):
                    along_x = (c == 0) != turned
                    groups.append(
                        [
                            (k * side + line if along_x else line * side + k) * mp_size + 2 * z + c
                            for k in range(side)
                        ]
                    )
        return groups

    def exchange(array, turned):
        flat = array.reshape(side, -1, LANES)
        return lax.all_to_all(
            flat, ("dp", "mp"), 0, 0, axis_index_groups=axis_groups(turned)
        ).reshape(array.shape)

    with jax.named_scope("norm"):
        copies = pl.pallas_call(
            norm_kernel,
            out_shape=jax.ShapeDtypeStruct((side, TILES + 1, rows, LANES), bf16),
            grid_spec=pltpu.PrefetchScalarGridSpec(
                num_scalar_prefetch=1,
                grid=(1,),
                in_specs=[
                    pl.BlockSpec((rows, D), lambda i, core: (0, 0)),
                    pl.BlockSpec((rows, HALF), lambda i, core: (0, core[0])),
                ],
                out_specs=whole((side, TILES + 1, rows, LANES)),
            ),
            compiler_params=roomy,
        )(core_scalar, hidden_state, hidden_state)

    with jax.named_scope("gather"):
        line = exchange(copies, False)
        line, critic_weight, policy_weight = lax.optimization_barrier(
            (line, critic_weight, policy_weight)
        )
        mine = exchange(jnp.broadcast_to(line[None], (side,) + line.shape), True).reshape(
            dp_size, TILES + 1, rows, LANES
        )
        weight_spec = pl.BlockSpec((CHUNK, width), lambda i: (i, 0))
        largest = pl.pallas_call(
            largest_kernel,
            out_shape=jax.ShapeDtypeStruct((1, width), f32),
            grid=(D // CHUNK,),
            in_specs=[weight_spec] * 2,
            out_specs=whole((1, width)),
            compiler_params=roomy,
            cost_estimate=pl.CostEstimate(
                flops=2**34, bytes_accessed=4 * D * width, transcendentals=0
            ),
        )(critic_weight, policy_weight)
        mine, largest = lax.optimization_barrier((mine, largest))
        other = swap(mine)

    state_block = (dp_size, CHUNK_TILES, rows, LANES)
    inverse_spec = pl.BlockSpec((dp_size, 1, rows, LANES), lambda i, *_: (0, TILES, 0, 0))

    def project(which, states, extra):
        last = bool(extra)
        weight_spec = pl.BlockSpec((CHUNK, width), lambda i, half, _: (half[0] * CHUNKS + i, 0))
        feature_spec = pl.BlockSpec((1, CHUNK), lambda i, half, _: (0, half[0] * CHUNKS + i))
        logits_shape = (tokens, 2 * width)
        out_shape = [jax.ShapeDtypeStruct(logits_shape, f32)]
        out_specs = [whole(logits_shape)]
        scratch = [pltpu.VMEM((tokens, CHUNK), bf16)]
        if last:
            out_shape += [
                jax.ShapeDtypeStruct((mp_size, 8, tokens), f32),
                jax.ShapeDtypeStruct((8, tokens), f32),
            ]
            out_specs += [whole((mp_size, 8, tokens)), whole((8, tokens))]
            scratch = [pltpu.VMEM((tokens, LANES), f32)] + scratch
        else:
            out_shape += [jax.ShapeDtypeStruct((tokens, LANES), f32)]
            out_specs += [whole((tokens, LANES))]
        return pl.pallas_call(
            functools.partial(project_kernel, last),
            out_shape=out_shape,
            grid_spec=pltpu.PrefetchScalarGridSpec(
                num_scalar_prefetch=2,
                grid=(CHUNKS,),
                in_specs=[
                    pl.BlockSpec(state_block, lambda i, *_: (0, i, 0, 0)),
                    inverse_spec,
                    feature_spec,
                    feature_spec,
                    weight_spec,
                    weight_spec,
                ]
                + [whole(array.shape) for array in extra],
                out_specs=out_specs,
                scratch_shapes=scratch,
            ),
            compiler_params=roomy,
            cost_estimate=pl.CostEstimate(
                flops=2 * tokens * HALF * 2 * width,
                bytes_accessed=2 * (2 * HALF * width + 2 * tokens * HALF),
                transcendentals=0,
            ),
        )(
            which,
            block_scalar,
            states,
            states,
            gain_row,
            value_row,
            critic_weight,
            policy_weight,
            *extra,
        )

    with jax.named_scope("logits"):
        sums, value_lanes = project(core_scalar, mine, [])
        logits, totals, own_rows = project(
            far_scalar, other, [sums, value_lanes, largest, info]
        )

    with jax.named_scope("totals"):
        totals = lax.all_to_all(totals, "mp", 0, 0)
        totals = pl.pallas_call(
            merge_kernel,
            out_shape=jax.ShapeDtypeStruct((dp_size, 8, tokens), f32),
            compiler_params=roomy,
        )(totals)
        totals = lax.all_to_all(totals, "dp", 0, 0)

    matmul_cost = pl.CostEstimate(
        flops=2 * tokens * HALF * 2 * width,
        bytes_accessed=2 * (2 * HALF * width + 2 * tokens * HALF),
        transcendentals=0,
    )
    part_shape = (dp_size, TILES + TILES // rows, rows, LANES)

    def part(which, states, extra, with_grads):
        def chunk(i):
            return jnp.minimum(i, CHUNKS - 1)

        weight_spec = pl.BlockSpec(
            (CHUNK, width), lambda i, half, _: (half[0] * CHUNKS + chunk(i), 0)
        )
        out_shape = [jax.ShapeDtypeStruct(part_shape, f32)]
        out_specs = [pl.BlockSpec(state_block, lambda i, *_: (0, i, 0, 0))]
        if with_grads:
            out_shape += [
                jax.ShapeDtypeStruct((tokens, 2 * width), bf16),
                jax.ShapeDtypeStruct((tokens, LANES), f32),
            ]
            out_specs += [whole((tokens, 2 * width)), whole((tokens, LANES))]
        return pl.pallas_call(
            functools.partial(part_kernel, with_grads),
            out_shape=out_shape,
            grid_spec=pltpu.PrefetchScalarGridSpec(
                num_scalar_prefetch=2,
                grid=(CHUNKS + 1,),
                in_specs=[whole(array.shape) for array in extra]
                + [
                    pl.BlockSpec(state_block, lambda i, *_: (0, chunk(i), 0, 0)),
                    inverse_spec,
                    weight_spec,
                    weight_spec,
                ],
                out_specs=out_specs,
                scratch_shapes=[pltpu.VMEM((TILES, LANES), f32)],
            ),
            compiler_params=roomy,
            cost_estimate=matmul_cost,
        )(which, block_scalar, *extra, states, states, critic_weight, policy_weight)

    with jax.named_scope("reduce"):
        part_other, grads, column = part(
            far_scalar, other, [totals, own_rows, info, logits], True
        )
        arrived = swap(part_other.astype(f16))
        (part_mine,) = part(core_scalar, mine, [grads, column], False)
        joined = (part_mine + arrived.astype(f32)).astype(f16)
        lines = exchange(joined.reshape((side, side) + part_shape[1:]), False)

    with jax.named_scope("weights"):

        def own_chunk(i):
            return jnp.minimum(i, CHUNKS - 1)

        def far_chunk(i):
            return jnp.maximum(i - CHUNKS, 0)

        def out_chunk(i, half):
            return jnp.where(
                i < CHUNKS, half[0] * CHUNKS + i, (1 - half[0]) * CHUNKS + i - CHUNKS
            )

        grad_critic, grad_value, extra = pl.pallas_call(
            weights_kernel,
            out_shape=[
                jax.ShapeDtypeStruct((D, width), bf16),
                jax.ShapeDtypeStruct((1, D), f32),
                jax.ShapeDtypeStruct((TILES, LANES), f32),
            ],
            grid_spec=pltpu.PrefetchScalarGridSpec(
                num_scalar_prefetch=1,
                grid=(2 * CHUNKS,),
                in_specs=[
                    pl.BlockSpec(state_block, lambda i, half: (0, own_chunk(i), 0, 0)),
                    inverse_spec,
                    pl.BlockSpec(state_block, lambda i, half: (0, far_chunk(i), 0, 0)),
                    inverse_spec,
                    pl.BlockSpec((1, CHUNK), lambda i, half: (0, out_chunk(i, half))),
                    pl.BlockSpec((tokens, width), lambda i, half: (0, 0)),
                    whole((tokens, LANES)),
                ],
                out_specs=[
                    pl.BlockSpec((CHUNK, width), lambda i, half: (out_chunk(i, half), 0)),
                    pl.BlockSpec((1, CHUNK), lambda i, half: (0, out_chunk(i, half))),
                    pl.BlockSpec((CHUNK_TILES, LANES), lambda i, half: (own_chunk(i), 0)),
                ],
                scratch_shapes=[pltpu.VMEM((tokens, CHUNK), bf16)],
            ),
            compiler_params=roomy,
            cost_estimate=pl.CostEstimate(
                flops=2 * tokens * D * width,
                bytes_accessed=2 * (D * width + 2 * tokens * D),
                transcendentals=0,
            ),
        )(core_scalar, mine, mine, other, other, gain_row, grads, column)
        far_extra = swap(extra)
        token = lax.dynamic_slice(column, (block_index, 0), (1, LANES))
        state_row = lax.dynamic_slice_in_dim(hidden_state, mp_index, 1, 0).reshape(
            2 * TILES, LANES
        )
        lines, grad_critic, grad_value, far_extra, token, state_row = lax.optimization_barrier(
            (lines, grad_critic, grad_value, far_extra, token, state_row)
        )

    with jax.named_scope("lines"):
        blocks = exchange(jnp.sum(lines.astype(f32), axis=0).astype(f16), True)

    with jax.named_scope("chips"):
        block = jnp.sum(blocks.astype(f32), axis=0).reshape(-1, LANES)
        shares = pl.pallas_call(
            split_kernel,
            out_shape=jax.ShapeDtypeStruct((chip_count, 3 * TILES, LANES), f32),
            compiler_params=roomy,
        )(block)
        shares = lax.all_to_all(
            shares.astype(f16), "mp", 0, 0, axis_index_groups=chip_groups
        )
        own = jnp.sum(shares.astype(f32), axis=0)
        far = swap(own)

    with jax.named_scope("finish"):
        smem = pl.BlockSpec(memory_space=pltpu.SMEM)
        vmem = pl.BlockSpec(memory_space=pltpu.VMEM)
        grad_hidden, grad_gain = pl.pallas_call(
            finish_kernel,
            out_shape=[
                jax.ShapeDtypeStruct((1, D), bf16),
                jax.ShapeDtypeStruct((2 * TILES, LANES), f32),
            ],
            in_specs=[smem] + [vmem] * 8,
            compiler_params=roomy,
        )(
            core_scalar,
            token,
            own,
            far,
            extra,
            far_extra,
            state_row,
            norm_gain.reshape(2 * TILES, LANES),
            value_weight.reshape(2 * TILES, LANES),
        )
    return (grad_hidden, grad_gain.reshape(D), grad_critic, grad_value.reshape(D))


def solution(mesh):
    placed = (
        P("dp", None),
        P(),
        P(None, ("dp", "mp")),
        P(None, ("dp", "mp")),
        P(),
        P(),
        P(),
        P(),
        P(),
    )
    return jax.shard_map(
        body,
        mesh=mesh,
        in_specs=placed,
        out_specs=(P(("dp", "mp"), None), P(), P(None, ("dp", "mp")), P()),
        check_vma=False,
    )
```

time: 602 us -> 142 us (0.24)
  waiting for transfers between devices: 322 us -> 18 us
  blocking collectives: 228 us -> 60.1 us
  Pallas kernels: 0 us -> 28.6 us
  matrix products: 25.9 us -> 0 us
  starting transfers between devices: 0.08 us -> 16.6 us
  between operations: 14.2 us -> 0.86 us
  local copies, waits for them, and re-layouts: 2.06 us -> 12.4 us
    unnamed x3 -> x0, waiting for transfers between devices: 263 us -> none
    psum x2 -> x0, blocking collectives: 152 us -> none  [the longest x1 77.6 us: body(): grad_gain = lax.psum(jnp.sum(normed_grad * own_unit, axis=0), ('dp', 'mp'))]
    pmax x1 -> x0, blocking collectives: 75.9 us -> none  [body(): critic_max, policy_max = lax.pmax((critic_top, policy_top), ('dp', 'mp'))]
    all_to_all x0 -> x5, blocking collectives: none -> 60.1 us  [the longest x2 21.7 us: exchange(): lax.all_to_all(flat, ('dp', 'mp'), 0, 0, axis_index_groups=axis_groups(tu...]
    all_gather x1 -> x0, waiting for transfers between devices: 59 us -> none  [body(): portion = lax.all_gather(normed_own, 'dp', axis=0, tiled=True)]
    pallas_call x0 -> x10, Pallas kernels: none -> 28.6 us  [the longest x1 9.63 us: body(): pl.pallas_call(weights_kernel, out_shape=[jax.ShapeDtypeStruct((D, width)...]
    dot_general x7 -> x0, matrix products: 25.9 us -> none  [the longest x2 8.35 us: contract_rows(): lax.dot_general(left_side, right_side, (((1,), (1,)), ((), ())), preferre...]
    all_to_all x0 -> x2, waiting for transfers between devices: none -> 15.6 us  [exchange(): lax.all_to_all(flat, ('dp', 'mp'), 0, 0, axis_index_groups=axis_groups(tu...]
  transfers between devices with their start and end apart: 2 -> 6, of which waited for: 2 -> 5; matrix products, arithmetic and copies ran while one was open for 2% -> 1% of each run, Pallas kernels for 0% -> 12%
where the time goes in v2:
time: 142 us; the launch traced here: 141 us
  blocking collectives  60.1 us (42%)
  Pallas kernels  28.6 us (20%)
  waiting for transfers between devices  18 us (13%)
  starting transfers between devices  16.6 us (12%)
  local copies, waits for them, and re-layouts  12.4 us (9%)
  other arithmetic  4.52 us (3%)
    all_to_all x2, blocking collectives, exchange(): lax.all_to_all(flat, ('dp', 'mp'), 0, 0, axis_index_groups=axis_groups(tu...  21.7 us
    all_to_all x1, blocking collectives, body(): totals = lax.all_to_all(totals, 'mp', 0, 0)  17.6 us
    all_to_all x2, waiting for transfers between devices, exchange(): lax.all_to_all(flat, ('dp', 'mp'), 0, 0, axis_index_groups=axis_groups(tu...  15.6 us
    all_to_all x1, blocking collectives, body(): lax.all_to_all(shares.astype(f16), 'mp', 0, 0, axis_index_groups=chip_gro...  11.1 us
    all_to_all x1, blocking collectives, body(): totals = lax.all_to_all(totals, 'dp', 0, 0)  9.82 us
    unnamed x26, local copies, waits for them, and re-layouts  9.73 us
    pallas_call x1, Pallas kernels, body(): pl.pallas_call(weights_kernel, out_shape=[jax.ShapeDtypeStruct((D, width)...  9.63 us
    pallas_call x2, Pallas kernels, project(): pl.pallas_call(functools.partial(project_kernel, last), out_shape=out_sha...  9.12 us
  transfers between devices with their start and end apart: 6, of which 5 were waited for; matrix products, arithmetic and copies ran while one was open for 1% of the time, Pallas kernels for 12%

profile of v2, /device:TPU:1, one launch (start us, length us, event | category | flops | bytes accessed | tf_op | source)
XLA Modules:
  0.0 141.2 jit_solution(3155769246892323653)
XLA Ops:
  0.6 0.0 copy-start.6
  0.7 0.9 copy-done.6
  1.6 0.2 norm.1
  1.8 11.9 %all_to_all.35 = bf16[4,528,128]{2,1,0:T(8,128)(2,1)S(1)} all-to-all(bf16[4,528,128]{2,1,0:T(8,128)(2,1)S(1)} %bitcast.25), channel_id=1, replica_groups={{0,64,128,192},{16,80,144,208},{32,96,160,224},{48,112,176,240},{2,66,1..., dimensions={0} | all-to-all | bytes 1081344 | tf_op jit(solution)/shard_map/gather/all_to_all | solution.py:476
  13.7 1.6 %broadcast_in_dim.9 = bf16[4,2112,128]{2,1,0:T(8,128)(2,1)} broadcast(bf16[2112,128]{1,0:T(8,128)(2,1)S(1)} %bitcast.31), dimensions={1,2} | broadcast | bytes 2703360 | tf_op jit(solution)/shard_map/gather/broadcast_in_dim | solution.py:501
  15.3 4.0 %all-to-all-start.1 = ((bf16[4,2112,128]{2,1,0:T(8,128)(2,1)}), bf16[4,2112,128]{2,1,0:T(8,128)(2,1)S(1)}, u32[]{:S(2)}, u32[]{:S(2)}) async-start(bf16[4,2112,128]{2,1,0:T(8,128)(2,1)} %broadcast_in_dim.9), calls=%async_computation.1 | async-start | bytes 4325376 | tf_op jit(solution)/shard_map/gather/all_to_all | solution.py:476
  19.2 0.0 copy-start
  19.2 2.2 %copy-done = bf16[8192,256]{1,0:T(8,128)(2,1)S(1)} copy-done((bf16[8192,256]{1,0:T(8,128)(2,1)S(1)}, bf16[8192,256]{1,0:T(8,128)(2,1)}, u32[]{:S(2)}) %copy-start) | copy-done | bytes 4194328
  21.4 0.0 copy-start.3
  21.4 2.2 %copy-done.3 = bf16[8192,256]{1,0:T(8,128)(2,1)S(1)} copy-done((bf16[8192,256]{1,0:T(8,128)(2,1)S(1)}, bf16[8192,256]{1,0:T(8,128)(2,1)}, u32[]{:S(2)}) %copy-start.3) | copy-done | bytes 4194328
  23.6 0.0 copy-start.7
  23.6 0.0 copy-start.8
  23.6 0.0 copy-start.9
  23.6 0.0 copy-start.10
  23.6 0.0 copy-start.11
  23.6 0.0 copy-start.12
  23.6 0.6 gather.1.rest_2_
  24.2 11.0 %all-to-all-done.1 = bf16[4,2112,128]{2,1,0:T(8,128)(2,1)S(1)} async-done(((bf16[4,2112,128]{2,1,0:T(8,128)(2,1)}), bf16[4,2112,128]{2,1,0:T(8,128)(2,1)S(1)}, u32[]{:S(2)}, u32[]{:S(2)}) %all-to-all-start.1) | async-done | bytes 2162720 | tf_op jit(solution)/shard_map/gather/all_to_all | solution.py:476
  35.2 3.2 %collective-permute-start = (bf16[16,33,16,128]{3,2,1,0:T(8,128)(2,1)S(1)}, bf16[16,33,16,128]{3,2,1,0:T(8,128)(2,1)}, u32[]{:S(2)}, u32[]{:S(2)}) collective-permute-start(bf16[16,33,16,128]{3,2,1,0:T(8,128)(2,1)S(1)} %bitcast.18), channel_id=1, source_target_pairs={{0,1},{1,0},{2,3},{3,2},{4,5},{5,4},{6,7},{7,6},{8,9},{9,8},{10,11... | collective-permute-start | bytes 6488072 | tf_op jit(solution)/shard_map/gather/ppermute | solution.py:452
  38.5 0.0 copy-done.7
  38.5 0.0 copy-done.8
  38.5 0.0 copy-done.9
  38.5 0.0 copy-done.10
  38.6 0.0 copy-done.11
  38.6 0.0 copy-done.12
  38.6 0.0 copy-start.1
  38.6 2.2 %copy-done.1 = bf16[8192,256]{1,0:T(8,128)(2,1)S(1)} copy-done((bf16[8192,256]{1,0:T(8,128)(2,1)S(1)}, bf16[8192,256]{1,0:T(8,128)(2,1)}, u32[]{:S(2)}) %copy-start.1) | copy-done | bytes 4194328
  40.8 0.0 copy-start.4
  40.8 2.2 %copy-done.4 = bf16[8192,256]{1,0:T(8,128)(2,1)S(1)} copy-done((bf16[8192,256]{1,0:T(8,128)(2,1)S(1)}, bf16[8192,256]{1,0:T(8,128)(2,1)}, u32[]{:S(2)}) %copy-start.4) | copy-done | bytes 4194328
  43.0 0.0 copy-start.2
  43.0 0.0 copy-start.5
  43.0 3.8 %logits.2 = (f32[256,512]{1,0:T(8,128)S(1)}, f32[256,128]{1,0:T(8,128)S(1)}) custom-call(s32[1]{0:T(128)} %bitcast.core_ref, s32[1]{0:T(128)} %bitcast.1.block_ref, bf16[16,33,16,128]{3,2,1,0:T(8,128)(2,1)S(1)} %bitcast.19, bf16[16,33,16,128]{3,2,1,0:T(8,128)(2,1)S(1)} %bitcast.20, bf16[1,8192]{1,0:T(2,128)(2,1)S(1)} %reshape.66.gain_ref, ...), custom_call_target="tpu_custom_call" | custom-call | flops 1073741824 | bytes 8388608 | tf_op jit(solution)/shard_map/logits/pallas_call | solution.py:540
  46.8 0.0 collective-permute-done.state_ref.inverse_ref.refs_4_.refs_5_.other_ref.other_inverse_ref
  46.9 0.0 copy-done.2
  46.9 0.0 copy-done.5
  46.9 5.3 %logits.3 = (f32[256,512]{1,0:T(8,128)S(1)}, f32[16,8,256]{2,1,0:T(8,128)S(1)}, f32[8,256]{1,0:T(8,128)S(1)}) custom-call(s32[1]{0:T(128)S(6)} %sub.3.core_ref, s32[1]{0:T(128)} %bitcast.1.block_ref, bf16[16,33,16,128]{3,2,1,0:T(8,128)(2,1)} %collective-permute-done.state_ref.inverse_ref.refs_4_.refs_5_.other_ref.other_inverse_ref, ...), custom_call_target="tpu_custom_call" | custom-call | flops 1073741824 | bytes 8388608 | tf_op jit(solution)/shard_map/logits/pallas_call | solution.py:540
  52.2 17.6 %all_to_all.36.parts_ref = f32[16,8,256]{2,1,0:T(8,128)S(1)} all-to-all(f32[16,8,256]{2,1,0:T(8,128)S(1)} %get-tuple-element.35), channel_id=1, replica_groups=mesh['dp'=16,'mp'=16] {'mp'}, dimensions={0} | all-to-all | bytes 262144 | tf_op jit(solution)/shard_map/totals/all_to_all | solution.py:583
  69.7 0.1 totals.1
  69.8 9.8 %all_to_all.37.refs_0_ = f32[16,8,256]{2,1,0:T(8,128)S(1)} all-to-all(f32[16,8,256]{2,1,0:T(8,128)S(1)} %totals.1), channel_id=1, replica_groups=mesh['dp'=16,'mp'=16] {'dp'}, dimensions={0} | all-to-all | bytes 262144 | tf_op jit(solution)/shard_map/totals/all_to_all | solution.py:589
  79.6 4.9 %reduce.5 = (f32[16,34,16,128]{3,2,1,0:T(8,128)S(1)}, bf16[256,512]{1,0:T(8,128)(2,1)S(1)}, f32[256,128]{1,0:T(8,128)S(1)}) custom-call(s32[1]{0:T(128)S(6)} %sub.3.core_ref, s32[1]{0:T(128)} %bitcast.1.block_ref, f32[16,8,256]{2,1,0:T(8,128)S(1)} %all_to_all.37.refs_0_, f32[8,256]{1,0:T(8,128)S(1)} %get-tuple-element.36.refs_1_, ...), custom_call_target="tpu_custom_call" | custom-call | flops 1073741824 | bytes 8388608 | tf_op jit(solution)/shard_map/reduce/pallas_call | solution.py:613
  84.5 0.3 convert_element_type.33
  84.8 1.1 collective-permute-start.1
  85.9 3.2 %reduce.6 = f32[16,34,16,128]{3,2,1,0:T(8,128)S(1)} custom-call(s32[1]{0:T(128)} %bitcast.core_ref, s32[1]{0:T(128)} %bitcast.1.block_ref, bf16[256,512]{1,0:T(8,128)(2,1)S(1)} %get-tuple-element.38.refs_0_.grads_ref, f32[256,128]{1,0:T(8,128)S(1)} %get-tuple-element.39.refs_1_.column_ref, bf16[16,33,16,128]{3,2,1,0:T(8,128)(2,1)S(1)} %bitcast.21, ...), custom_call_target="tpu_custom_call" | custom-call | flops 1073741824 | bytes 8388608 | tf_op jit(solution)/shard_map/reduce/pallas_call | solution.py:613
  89.1 0.8 collective-permute-done.1
  89.8 1.9 %add_convert_fusion = f16[16,34,16,128]{3,2,1,0:T(8,128)(2,1)} fusion(f32[16,34,16,128]{3,2,1,0:T(8,128)S(1)} %reduce.6, f16[16,34,16,128]{3,2,1,0:T(8,128)(2,1)S(1)} %collective-permute-done.1), kind=kLoop, calls=%fused_computation.1 | loop fusion | flops 3342336 | bytes 8912896 | tf_op jit(solution)/shard_map/reduce/convert_element_type | solution.py:639
  91.8 4.5 %all-to-all-start.4 = ((f16[4,2176,128]{2,1,0:T(8,128)(2,1)}), f16[4,2176,128]{2,1,0:T(8,128)(2,1)}, u32[]{:S(2)}, u32[]{:S(2)}) async-start(f16[4,2176,128]{2,1,0:T(8,128)(2,1)} %bitcast.29), calls=%async_computation.4 | async-start | bytes 4456448 | tf_op jit(solution)/shard_map/reduce/all_to_all | solution.py:476
  96.2 1.0 dynamic-slice_reduce_fusion
  97.3 9.6 %weights.1 = (bf16[8192,256]{1,0:T(8,128)(2,1)}, f32[1,8192]{1,0:T(1,128)}, f32[32,128]{1,0:T(8,128)S(1)}) custom-call(s32[1]{0:T(128)} %bitcast.core_ref, bf16[16,33,16,128]{3,2,1,0:T(8,128)(2,1)S(1)} %bitcast.23, bf16[16,33,16,128]{3,2,1,0:T(8,128)(2,1)S(1)} %bitcast.24, ...), custom_call_target="tpu_custom_call" | custom-call | flops 1073741824 | bytes 12582912 | tf_op jit(solution)/shard_map/weights/pallas_call | solution.py:655
  106.9 0.4 collective-permute-start.2
  107.3 0.8 collective-permute-done.2.far_extra_ref
  108.1 4.5 %all-to-all-done.4 = f16[4,2176,128]{2,1,0:T(8,128)(2,1)} async-done(((f16[4,2176,128]{2,1,0:T(8,128)(2,1)}), f16[4,2176,128]{2,1,0:T(8,128)(2,1)}, u32[]{:S(2)}, u32[]{:S(2)}) %all-to-all-start.4) | async-done | bytes 2228256 | tf_op jit(solution)/shard_map/reduce/all_to_all | solution.py:476
  112.7 2.1 %convert_reduce_fusion = f32[4,34,16,128]{3,2,1,0:T(8,128)S(1)} fusion(f16[4,4,34,16,128]{4,3,2,1,0:T(8,128)(2,1)} %bitcast.11), kind=kLoop, calls=%fused_computation | loop fusion | flops 1949696 | bytes 3342336 | tf_op jit(solution)/shard_map/lines/reduce_sum | solution.py:698
  114.8 0.1 convert_element_type.37
  114.8 9.8 %all_to_all.38 = f16[4,544,128]{2,1,0:T(8,128)(2,1)S(1)} all-to-all(f16[4,544,128]{2,1,0:T(8,128)(2,1)S(1)} %bitcast.30), channel_id=1, replica_groups={{0,16,32,48},{64,80,96,112},{128,144,160,176},{192,208,224,240},{2,18,3..., dimensions={0} | all-to-all | bytes 1114112 | tf_op jit(solution)/shard_map/lines/all_to_all | solution.py:476
  124.6 0.1 convert_reduce_fusion.1.block_ref
  124.7 0.1 chips.1
  124.8 11.1 %all_to_all.39 = f16[8,96,128]{2,1,0:T(8,128)(2,1)S(1)} all-to-all(f16[8,96,128]{2,1,0:T(8,128)(2,1)S(1)} %convert_element_type.40), channel_id=1, replica_groups={{0,2,4,6,8,10,12,14},{1,3,5,7,9,11,13,15},{16,18,20,22,24,26,28,30},{17..., dimensions={0} | all-to-all | bytes 393216 | tf_op jit(solution)/shard_map/chips/all_to_all | solution.py:707
  135.9 3.5 %collective-permute-start.3 = (f32[96,128]{1,0:T(8,128)S(1)}, f32[96,128]{1,0:T(8,128)S(1)}, u32[]{:S(2)}, u32[]{:S(2)}) collective-permute-start(f32[96,128]{1,0:T(8,128)S(1)} %convert_reduce_fusion.2.own_ref), channel_id=1, source_target_pairs={{0,1},{1,0},{2,3},{3,2},{4,5},{5,4},{6,7},{7,6},{8,9},{9,8},{10,11... | collective-permute-start | bytes 147464 | tf_op jit(solution)/shard_map/chips/ppermute | solution.py:452
  139.4 0.9 collective-permute-done.3.far_ref
  140.3 0.9 finish.1
  (7 shorter events, 0.1 us)
Async XLA Ops:
  0.6 1.0 copy-start.6
  15.3 20.0 %all-to-all-start.1 = ((bf16[4,2112,128]{2,1,0:T(8,128)(2,1)}), bf16[4,2112,128]{2,1,0:T(8,128)(2,1)S(1)}, u32[]{:S(2)}, u32[]{:S(2)}) async-start(bf16[4,2112,128]{2,1,0:T(8,128)(2,1)} %broadcast_in_dim.9), calls=%async_computation.1 | async-start | bytes 4325376 | tf_op jit(solution)/shard_map/gather/all_to_all | solution.py:476
  19.2 2.2 %copy-start = (bf16[8192,256]{1,0:T(8,128)(2,1)S(1)}, bf16[8192,256]{1,0:T(8,128)(2,1)}, u32[]{:S(2)}) copy-start(bf16[8192,256]{1,0:T(8,128)(2,1)} %refs_4_) | copy-start | bytes 12582916
  21.4 2.2 %copy-start.3 = (bf16[8192,256]{1,0:T(8,128)(2,1)S(1)}, bf16[8192,256]{1,0:T(8,128)(2,1)}, u32[]{:S(2)}) copy-start(bf16[8192,256]{1,0:T(8,128)(2,1)} %refs_5_) | copy-start | bytes 12582916
  23.6 14.9 %copy-start.7 = (bf16[8192]{0:T(1024)(128)(2,1)S(1)}, bf16[8192]{0:T(1024)(128)(2,1)}, u32[]{:S(2)}) copy-start(bf16[8192]{0:T(1024)(128)(2,1)} %param.10) | copy-start | bytes 49156
  23.6 14.9 %copy-start.8 = (bf16[8192]{0:T(1024)(128)(2,1)S(1)}, bf16[8192]{0:T(1024)(128)(2,1)}, u32[]{:S(2)}) copy-start(bf16[8192]{0:T(1024)(128)(2,1)} %param.13) | copy-start | bytes 49156
  23.6 14.9 %copy-start.9 = (s32[256]{0:T(256)S(1)}, s32[256]{0:T(256)}, u32[]{:S(2)}) copy-start(s32[256]{0:T(256)} %param.17) | copy-start | bytes 3076
  23.6 14.9 %copy-start.10 = (s32[256]{0:T(256)S(1)}, s32[256]{0:T(256)}, u32[]{:S(2)}) copy-start(s32[256]{0:T(256)} %param.14) | copy-start | bytes 3076
  23.6 14.9 %copy-start.11 = (s32[256]{0:T(256)S(1)}, s32[256]{0:T(256)}, u32[]{:S(2)}) copy-start(s32[256]{0:T(256)} %param.15) | copy-start | bytes 3076
  23.6 14.9 %copy-start.12 = (s32[256]{0:T(256)S(1)}, s32[256]{0:T(256)}, u32[]{:S(2)}) copy-start(s32[256]{0:T(256)} %param.16) | copy-start | bytes 3076
  35.2 11.6 %collective-permute-start = (bf16[16,33,16,128]{3,2,1,0:T(8,128)(2,1)S(1)}, bf16[16,33,16,128]{3,2,1,0:T(8,128)(2,1)}, u32[]{:S(2)}, u32[]{:S(2)}) collective-permute-start(bf16[16,33,16,128]{3,2,1,0:T(8,128)(2,1)S(1)} %bitcast.18), channel_id=1, source_target_pairs={{0,1},{1,0},{2,3},{3,2},{4,5},{5,4},{6,7},{7,6},{8,9},{9,8},{10,11... | collective-permute-start | bytes 6488072 | tf_op jit(solution)/shard_map/gather/ppermute | solution.py:452
  38.6 2.2 %copy-start.1 = (bf16[8192,256]{1,0:T(8,128)(2,1)S(1)}, bf16[8192,256]{1,0:T(8,128)(2,1)}, u32[]{:S(2)}) copy-start(bf16[8192,256]{1,0:T(8,128)(2,1)} %refs_4_) | copy-start | bytes 12582916
  40.8 2.2 %copy-start.4 = (bf16[8192,256]{1,0:T(8,128)(2,1)S(1)}, bf16[8192,256]{1,0:T(8,128)(2,1)}, u32[]{:S(2)}) copy-start(bf16[8192,256]{1,0:T(8,128)(2,1)} %refs_5_) | copy-start | bytes 12582916
  43.0 3.9 %copy-start.2 = (bf16[8192,256]{1,0:T(8,128)(2,1)S(1)}, bf16[8192,256]{1,0:T(8,128)(2,1)}, u32[]{:S(2)}) copy-start(bf16[8192,256]{1,0:T(8,128)(2,1)} %refs_4_) | copy-start | bytes 12582916
  43.0 3.9 %copy-start.5 = (bf16[8192,256]{1,0:T(8,128)(2,1)S(1)}, bf16[8192,256]{1,0:T(8,128)(2,1)}, u32[]{:S(2)}) copy-start(bf16[8192,256]{1,0:T(8,128)(2,1)} %refs_5_) | copy-start | bytes 12582916
  84.8 5.1 %collective-permute-start.1 = (f16[16,34,16,128]{3,2,1,0:T(8,128)(2,1)S(1)}, f16[16,34,16,128]{3,2,1,0:T(8,128)(2,1)S(1)}, u32[]{:S(2)}, u32[]{:S(2)}) collective-permute-start(f16[16,34,16,128]{3,2,1,0:T(8,128)(2,1)S(1)} %convert_element_type.33), channel_id=1, source_target_pairs={{0,1},{1,0},{2,3},{3,2},{4,5},{5,4},{6,7},{7,6},{8,9},{9,8},{10,11... | collective-permute-start | bytes 6684680 | tf_op jit(solution)/shard_map/reduce/ppermute | solution.py:452
  91.8 20.9 %all-to-all-start.4 = ((f16[4,2176,128]{2,1,0:T(8,128)(2,1)}), f16[4,2176,128]{2,1,0:T(8,128)(2,1)}, u32[]{:S(2)}, u32[]{:S(2)}) async-start(f16[4,2176,128]{2,1,0:T(8,128)(2,1)} %bitcast.29), calls=%async_computation.4 | async-start | bytes 4456448 | tf_op jit(solution)/shard_map/reduce/all_to_all | solution.py:476
  106.9 1.2 collective-permute-start.2
  135.9 4.4 %collective-permute-start.3 = (f32[96,128]{1,0:T(8,128)S(1)}, f32[96,128]{1,0:T(8,128)S(1)}, u32[]{:S(2)}, u32[]{:S(2)}) collective-permute-start(f32[96,128]{1,0:T(8,128)S(1)} %convert_reduce_fusion.2.own_ref), channel_id=1, source_target_pairs={{0,1},{1,0},{2,3},{3,2},{4,5},{5,4},{6,7},{7,6},{8,9},{9,8},{10,11... | collective-permute-start | bytes 147464 | tf_op jit(solution)/shard_map/chips/ppermute | solution.py:452

commit v3 on v2

v3 whole, which is shorter than its diff:
```python
import functools
import math

import jax
import jax.numpy as jnp
from jax import lax
from jax.experimental import pallas as pl
from jax.experimental.pallas import tpu as pltpu
from jax.sharding import PartitionSpec as P

D = 8192
HALF = D // 2
LANES = 128
TILES = HALF // LANES
CHUNK_TILES = 8
CHUNK = CHUNK_TILES * LANES
CHUNKS = TILES // CHUNK_TILES


discount = 0.99
expectile = 0.7
conservative = 0.5
reward_step = 0.5
epsilon = 1e-05
unit_limit = 91.0
half_limit = 32768.0

f32 = jnp.float32
bf16 = jnp.bfloat16
f16 = jnp.float16

roomy = pltpu.CompilerParams(vmem_limit_bytes=14 * 1024 * 1024)


def whole(shape):
    return pl.BlockSpec(shape, lambda *_: (0,) * len(shape))


def to_columns(rows):
    tokens = rows.shape[1]
    filled = jnp.concatenate([rows, jnp.zeros((LANES - rows.shape[0], tokens), f32)], axis=0)
    return jnp.transpose(filled)


def lane_pack(columns):
    tokens = columns[0].shape[0]
    lane = lax.broadcasted_iota(jnp.int32, (tokens, LANES), 1)
    packed = jnp.zeros((tokens, LANES), f32)
    for k, column in enumerate(columns):
        packed = jnp.where(lane == k, column, packed)
    return packed


def half_of(where_ref):
    return lax.rem(where_ref[0], 2)


def gathered_place(where_ref, group, side):
    own = lax.div(where_ref[0], 2)
    x, y = divmod(group, side)
    return jnp.where(
        half_of(where_ref) == 0,
        y * side + lax.rem(x - lax.div(own, side) + side, side),
        x * side + lax.rem(y - lax.rem(own, side) + side, side),
    )


def reduced_place(half, group, side):
    x, y = divmod(group, side)
    return jnp.where(half == 0, x * side + y, y * side + x)


def group_rows(group, rows):
    return slice(group * rows, (group + 1) * rows)


def spread_inverse(where_ref, inverse_ref, out_ref):
    groups, _, rows, _ = inverse_ref.shape
    side = math.isqrt(groups)
    for group in range(groups):
        parts = inverse_ref[gathered_place(where_ref, group, side), 0].astype(f32)
        inverse = parts[:, 0:1] + parts[:, 1:2] + parts[:, 2:3]
        out_ref[group_rows(group, rows)] = jnp.broadcast_to(inverse, (rows, LANES))


def norm_kernel(core_ref, state_ref, half_ref, out_ref):
    state = state_ref[...].astype(f32)
    mean = jnp.sum(state * state, axis=1, keepdims=True) / D
    inverse = lax.rsqrt(mean + epsilon)
    high = inverse.astype(bf16).astype(f32)
    middle = (inverse - high).astype(bf16).astype(f32)
    low = inverse - high - middle
    packed = lane_pack([high, middle, low]).astype(bf16)
    for tile in range(TILES):
        out_ref[tile] = half_ref[:, tile * LANES : (tile + 1) * LANES]
    out_ref[TILES] = packed


def column_tops(weight):
    width = weight.shape[1]
    largest = jnp.max(jnp.abs(weight).reshape(-1, 16, width), axis=0).astype(f32)
    return jnp.max(largest, axis=0, keepdims=True)


def gather_sum(step, ref, part):
    @pl.when(step == 0)
    def _():
        ref[...] = part

    @pl.when(step > 0)
    def _():
        ref[...] += part


def gather_top(step, ref, part):
    @pl.when(step == 0)
    def _():
        ref[...] = part

    @pl.when(step > 0)
    def _():
        ref[...] = jnp.maximum(ref[...], part)


def normed_chunk(core_ref, state_ref, inverse_ref, gain_ref, value_ref, normed_ref, spread, acc):
    step = pl.program_id(0)
    half = half_of(core_ref)
    groups, _, rows, _ = state_ref.shape
    side = math.isqrt(groups)

    @pl.when(step == 0)
    def _():
        spread_inverse(core_ref, inverse_ref, spread)
        acc[...] = jnp.zeros_like(acc)

    gains, values = [], []
    for tile in range(CHUNK_TILES):
        where = slice(tile * LANES, (tile + 1) * LANES)
        gains.append(gain_ref[:, where].astype(f32))
        values.append(value_ref[:, where].astype(f32))
    for group in range(groups):
        place = gathered_place(core_ref, group, side)
        lines = group_rows(group, rows)
        inverse = spread[lines]
        part = acc[lines]
        for tile in range(CHUNK_TILES):
            unit = state_ref[place, tile].astype(f32) * inverse
            normed = (unit * gains[tile]).astype(bf16)
            normed_ref[lines, tile * LANES : (tile + 1) * LANES] = normed
            part = part + normed.astype(f32) * values[tile]
        acc[lines] = part


def normed_kernel(
    core_ref, state_ref, inverse_ref, gain_ref, value_ref, normed_ref, value_acc, spread
):
    normed_chunk(
        core_ref, state_ref, inverse_ref, gain_ref, value_ref, normed_ref, spread, value_acc
    )


def head_kernel(core_ref, normed_ref, weight_ref, sums_ref, top_ref):
    step = pl.program_id(0)
    part = jnp.dot(normed_ref[...], weight_ref[...], preferred_element_type=f32)
    gather_sum(step, sums_ref, part)
    gather_top(step, top_ref, column_tops(weight_ref[...]))


def totals_kernel(
    core_ref,
    block_ref,
    state_ref,
    inverse_ref,
    gain_ref,
    value_ref,
    critic_ref,
    policy_ref,
    critic_in,
    policy_in,
    value_in,
    critic_top_in,
    policy_top_in,
    info_ref,
    powers_ref,
    totals_ref,
    own_ref,
    value_acc,
    top_ref,
    normed_ref,
    spread,
):
    step = pl.program_id(0)
    tokens = normed_ref.shape[0]
    width = critic_ref.shape[1]
    normed_chunk(
        core_ref, state_ref, inverse_ref, gain_ref, value_ref, normed_ref, spread, value_acc
    )
    critic = jnp.dot(normed_ref[...], critic_ref[...], preferred_element_type=f32)
    policy = jnp.dot(normed_ref[...], policy_ref[...], preferred_element_type=f32)
    gather_top(
        step, top_ref, jnp.maximum(column_tops(critic_ref[...]), column_tops(policy_ref[...]))
    )

    @pl.when(step == 0)
    def _():
        powers_ref[:, :width] = critic_in[...] + critic
        powers_ref[:, width:] = policy_in[...] + policy

    @pl.when(step > 0)
    def _():
        powers_ref[:, :width] += critic
        powers_ref[:, width:] += policy

    @pl.when(step == CHUNKS - 1)
    def _():
        critic_logits = powers_ref[:, :width]
        policy_logits = powers_ref[:, width:]
        critic_top = jnp.max(critic_logits, axis=1, keepdims=True)
        policy_top = jnp.max(policy_logits, axis=1, keepdims=True)
        column = lax.broadcasted_iota(jnp.int32, (tokens, width), 1) + block_ref[0] * width
        action = to_columns(info_ref[...])[:, 0:1].astype(jnp.int32)
        taken = jnp.sum(jnp.where(column == action, critic_logits, 0.0), axis=1, keepdims=True)
        critic_powers = jnp.exp(critic_logits - critic_top)
        policy_powers = jnp.exp(policy_logits - policy_top)
        powers_ref[:, :width] = critic_powers
        powers_ref[:, width:] = policy_powers
        value = jnp.sum(value_in[...], axis=1, keepdims=True) + jnp.sum(
            value_acc[...], axis=1, keepdims=True
        )
        top = jnp.maximum(top_ref[...], jnp.maximum(critic_top_in[...], policy_top_in[...]))
        weight_top = jnp.broadcast_to(jnp.max(top, axis=1, keepdims=True), (tokens, 1))
        packed = jnp.transpose(
            lane_pack(
                [
                    critic_top,
                    policy_top,
                    jnp.sum(critic_powers, axis=1, keepdims=True),
                    jnp.sum(policy_powers, axis=1, keepdims=True),
                    taken,
                    weight_top,
                    value,
                ]
            )
        )[:8]
        own_ref[...] = packed
        for copy in range(totals_ref.shape[0]):
            totals_ref[copy] = packed


def merge_parts(parts):
    tops = parts[:, 0:2]
    top = jnp.max(tops, axis=0)
    total = jnp.sum(parts[:, 2:4] * jnp.exp(tops - top[None]), axis=0)
    taken = jnp.sum(parts[:, 4:5], axis=0)
    weight_top = jnp.max(parts[:, 5:6], axis=0)
    return top, total, taken, weight_top


def merge_kernel(parts_ref, out_ref):
    tokens = parts_ref.shape[2]
    packed = jnp.concatenate([*merge_parts(parts_ref[...]), jnp.zeros((2, tokens), f32)], axis=0)
    for copy in range(out_ref.shape[0]):
        out_ref[copy] = packed


def turn(left, right):
    return lax.dot_general(left, right, (((1,), (1,)), ((), ())), preferred_element_type=f32)


def part_kernel(with_grads, core_ref, block_ref, *refs):
    if with_grads:
        parts_ref, own_ref, info_ref, powers_ref, *refs = refs
        state_ref, inverse_ref, critic_ref, policy_ref, out_ref, grads_ref, column_ref, *refs = refs
    else:
        grads_ref, column_ref, *refs = refs
        state_ref, inverse_ref, critic_ref, policy_ref, out_ref, *refs = refs
    gain_acc, spread, scales = refs
    step = pl.program_id(0)
    tokens = grads_ref.shape[0]
    width = critic_ref.shape[1]
    groups, _, rows, _ = out_ref.shape

    if with_grads:

        @pl.when(step == 0)
        def _():
            top, total, critic_taken, weight_top = merge_parts(parts_ref[...])
            values = own_ref[6:7]
            action, reward, done, live = (info_ref[k : k + 1] for k in range(4))
            place = lax.broadcasted_iota(jnp.int32, (1, tokens), 1)
            next_values = jnp.where(place == tokens - 1, 0.0, pltpu.roll(values, tokens - 1, 1))
            target = reward_step * reward + discount * (1.0 - done) * next_values
            advantage = critic_taken - values
            weights = jnp.where(advantage >= 0.0, expectile, 1.0 - expectile)
            value_coef = live * -2.0 * weights * advantage
            critic_coef = live * (2.0 * (critic_taken - target) - conservative)
            bound = (2.5 + jnp.abs(critic_coef)) * jnp.maximum(weight_top, 1e-20)
            gain_bound = jnp.sum(bound, axis=1, keepdims=True) * unit_limit
            first = to_columns(
                jnp.concatenate(
                    [
                        value_coef,
                        half_limit / bound,
                        bound / half_limit,
                        jnp.broadcast_to(half_limit / gain_bound, (1, tokens)),
                        jnp.broadcast_to(gain_bound / half_limit, (1, tokens)),
                        critic_coef,
                        action,
                        live,
                    ],
                    axis=0,
                )
            )
            column_ref[...] = first
            second = to_columns(
                jnp.concatenate(
                    [jnp.exp(own_ref[0:2] - top) / total, jnp.zeros((6, tokens), f32)], axis=0
                )
            )
            coef = first[:, 5:6]
            live_column = first[:, 7:8]
            column = lax.broadcasted_iota(jnp.int32, (tokens, width), 1) + block_ref[0] * width
            chosen = (column == first[:, 6:7].astype(jnp.int32)).astype(f32)
            critic_probs = powers_ref[:, :width] * second[:, 0:1]
            policy_probs = powers_ref[:, width:] * second[:, 1:2]
            grads_ref[:, :width] = (
                conservative * live_column * critic_probs + coef * chosen
            ).astype(bf16)
            grads_ref[:, width:] = (live_column * (policy_probs - chosen)).astype(bf16)

    half = half_of(core_ref)
    side = math.isqrt(groups)

    @pl.when(step == 0)
    def _():
        spread_inverse(core_ref, inverse_ref, spread)
        scales[...] = jnp.broadcast_to(column_ref[:, 1:2], scales.shape)

    @pl.when(step < CHUNKS)
    def _():
        part = turn(grads_ref[:, :width], critic_ref[...]) + turn(
            grads_ref[:, width:], policy_ref[...]
        )
        scale = scales[...]
        inverse = spread[...]
        gains = []
        for tile in range(CHUNK_TILES):
            block = part[:, tile * LANES : (tile + 1) * LANES]
            scaled = block * scale
            for group in range(groups):
                out_ref[reduced_place(half, group, side), tile] = scaled[group_rows(group, rows)]
            state = jnp.concatenate(
                [
                    state_ref[gathered_place(core_ref, group, side), tile].astype(f32)
                    for group in range(groups)
                ],
                axis=0,
            )
            gains.append(jnp.sum(block * (state * inverse), axis=0, keepdims=True))
        gain_acc[pl.ds(pl.multiple_of(step * CHUNK_TILES, CHUNK_TILES), CHUNK_TILES)] = (
            jnp.concatenate(gains, axis=0)
        )

    @pl.when(step == CHUNKS)
    def _():
        gain = (gain_acc[...] * column_ref[0:1, 3:4]).reshape(TILES // rows, rows, LANES)
        for group in range(groups):
            out_ref[group, : TILES // rows] = gain


def weights_kernel(far, core_ref, state_ref, inverse_ref, gain_ref, grads_ref, column_ref, *refs):
    if far:
        _, _, critic_ref, value_ref, normed_ref, spread, coefs = refs
    else:
        critic_ref, value_ref, extra_ref, normed_ref, spread, coefs = refs
    step = pl.program_id(0)
    half = half_of(core_ref)
    groups, _, rows, _ = state_ref.shape
    side = math.isqrt(groups)

    @pl.when(step == 0)
    def _():
        spread_inverse(core_ref, inverse_ref, spread)
        coefs[...] = jnp.broadcast_to(column_ref[:, 0:1], coefs.shape)

    extras = []
    for tile in range(CHUNK_TILES):
        where = slice(tile * LANES, (tile + 1) * LANES)
        gain = gain_ref[:, where].astype(f32)
        value = jnp.zeros((rows, LANES), f32)
        extra = jnp.zeros((rows, LANES), f32)
        for group in range(groups):
            lines = group_rows(group, rows)
            state = state_ref[gathered_place(core_ref, group, side), tile].astype(f32)
            unit = state * spread[lines]
            normed = (unit * gain).astype(bf16)
            normed_ref[lines, where] = normed
            coef = coefs[lines]
            value = value + normed.astype(f32) * coef
            extra = extra + unit * coef
        value_ref[:, where] = jnp.sum(value, axis=0, keepdims=True)
        extras.append(jnp.sum(extra, axis=0, keepdims=True))
    critic_ref[...] = lax.dot_general(
        normed_ref[...], grads_ref[...], (((0,), (0,)), ((), ())), preferred_element_type=f32
    ).astype(bf16)
    if not far:
        extra_ref[...] = jnp.concatenate(extras, axis=0)


def split_kernel(block_ref, out_ref):
    peers = out_ref.shape[0]
    rows = 2 * peers
    for peer in range(peers):
        for k in range(2):
            out_ref[peer, k * TILES : (k + 1) * TILES] = block_ref[
                pl.ds(2 * peer + k, TILES, stride=rows)
            ]
        out_ref[peer, 2 * TILES :] = block_ref[TILES * rows :]


def finish_kernel(
    core_ref,
    column_ref,
    own_ref,
    far_ref,
    own_extra_ref,
    far_extra_ref,
    state_ref,
    weight_ref,
    value_ref,
    hidden_ref,
    gain_ref,
):
    first = half_of(core_ref) == 0
    own_half = jnp.where(first, own_ref[:TILES], own_ref[TILES : 2 * TILES])
    far_half = jnp.where(first, far_ref[:TILES], far_ref[TILES : 2 * TILES])
    row = jnp.concatenate(
        [jnp.where(first, own_half, far_half), jnp.where(first, far_half, own_half)], axis=0
    )
    value_coef = column_ref[:, 0:1]
    row_back = column_ref[:, 2:3]
    gain_back = column_ref[:, 4:5]
    value = value_ref[...].astype(f32)
    own_gain = own_ref[2 * TILES :] * gain_back
    far_gain = far_ref[2 * TILES :] * gain_back
    own_extra = own_extra_ref[...]
    far_extra = far_extra_ref[...]
    gain_ref[:TILES] = (
        jnp.where(first, own_gain, far_gain)
        + jnp.where(first, own_extra, far_extra) * value[:TILES]
    )
    gain_ref[TILES:] = (
        jnp.where(first, far_gain, own_gain)
        + jnp.where(first, far_extra, own_extra) * value[TILES:]
    )
    state = state_ref[...].astype(f32)
    mean = jnp.sum(jnp.sum(state * state, axis=1, keepdims=True), axis=0, keepdims=True) / D
    inverse = lax.rsqrt(mean + epsilon)
    unit = state * inverse
    normed_grad = row * row_back + value_coef * value
    scaled = normed_grad * weight_ref[...].astype(f32)
    row_dot = jnp.sum(jnp.sum(scaled * unit, axis=1, keepdims=True), axis=0, keepdims=True)
    grad = inverse * (scaled - unit * row_dot / D)
    for tile in range(2 * TILES):
        hidden_ref[:, tile * LANES : (tile + 1) * LANES] = grad[tile : tile + 1].astype(bf16)


def contract_tokens(left_side, right_side):
    return lax.dot_general(
        left_side, right_side, (((0,), (0,)), ((), ())), preferred_element_type=f32
    )


def body(
    hidden_state,
    norm_gain,
    critic_weight,
    policy_weight,
    value_weight,
    actions,
    rewards,
    done_flags,
    pad_mask,
):
    dp_size = lax.axis_size("dp")
    mp_size = lax.axis_size("mp")
    chip_count = mp_size // 2
    dp_index = lax.axis_index("dp")
    mp_index = lax.axis_index("mp")
    core = mp_index % 2
    core_swap = [(i, i ^ 1) for i in range(mp_size)]
    chip_groups = [[c + 2 * k for k in range(chip_count)] for c in range(2)]
    rows = hidden_state.shape[0]
    tokens = rows * dp_size
    width = critic_weight.shape[1]
    block_index = dp_index * mp_size + mp_index
    side = math.isqrt(dp_size)
    def scalars(half):
        return (half + 2 * dp_index).astype(jnp.int32).reshape(1)

    core_scalar = scalars(core)
    far_scalar = scalars(1 - core)
    block_scalar = block_index.astype(jnp.int32).reshape(1)

    def swap(array):
        return lax.ppermute(array, "mp", core_swap)

    gain_row = norm_gain.reshape(1, D)
    value_row = value_weight.reshape(1, D)
    info = jnp.stack([actions, rewards, done_flags, pad_mask] + [pad_mask] * 4).astype(f32)

    def axis_groups(turned):
        groups = []
        for c in range(2):
            for z in range(chip_count):
                for line in range(side):
                    along_x = (c == 0) != turned
                    groups.append(
                        [
                            (k * side + line if along_x else line * side + k) * mp_size + 2 * z + c
                            for k in range(side)
                        ]
                    )
        return groups

    def shift(array, step):
        moves = []
        for dp in range(dp_size):
            x, y = divmod(dp, side)
            for mp in range(mp_size):
                if mp % 2 == 0:
                    target = (x + step) % side * side + y
                else:
                    target = x * side + (y + step) % side
                moves.append((dp * mp_size + mp, target * mp_size + mp))
        return lax.ppermute(array, ("dp", "mp"), moves)

    def exchange(array, turned):
        flat = array.reshape(side, -1, LANES)
        return lax.all_to_all(
            flat, ("dp", "mp"), 0, 0, axis_index_groups=axis_groups(turned)
        ).reshape(array.shape)

    def pack(array, is_row):
        squared = array * jnp.abs(array) * (1.0 / half_limit)
        return jnp.where(is_row, squared, array).astype(f16)

    def unpack(array, is_row):
        array = array.astype(f32)
        root = jnp.sqrt(jnp.abs(array) * half_limit)
        return jnp.where(is_row, jnp.where(array < 0.0, -root, root), array)

    tile_is_row = jnp.arange(TILES + TILES // rows)[:, None, None] < TILES
    share_is_row = jnp.arange(3 * TILES)[:, None] < 2 * TILES
    tile_is_row = jnp.broadcast_to(tile_is_row, (TILES + TILES // rows, rows, LANES))
    share_is_row = jnp.broadcast_to(share_is_row, (3 * TILES, LANES))

    with jax.named_scope("norm"):
        payload = pl.pallas_call(
            norm_kernel,
            out_shape=jax.ShapeDtypeStruct((TILES + 1, rows, LANES), bf16),
            grid_spec=pltpu.PrefetchScalarGridSpec(
                num_scalar_prefetch=1,
                grid=(1,),
                in_specs=[
                    pl.BlockSpec((rows, D), lambda i, core: (0, 0)),
                    pl.BlockSpec((rows, HALF), lambda i, core: (0, half_of(core))),
                ],
                out_specs=whole((TILES + 1, rows, LANES)),
            ),
            compiler_params=roomy,
        )(core_scalar, hidden_state, hidden_state)

    with jax.named_scope("gather"):
        line = jnp.stack([payload] + [shift(payload, -step) for step in range(1, side)])
        mine = exchange(jnp.broadcast_to(line[None], (side,) + line.shape), True).reshape(
            dp_size, TILES + 1, rows, LANES
        )
        other = swap(mine)

    state_block = (dp_size, CHUNK_TILES, rows, LANES)
    inverse_spec = pl.BlockSpec((dp_size, 1, rows, LANES), lambda i, *_: (0, TILES, 0, 0))

    logits_cost = pl.CostEstimate(
        flops=2 * tokens * HALF * width,
        bytes_accessed=2 * HALF * (width + tokens),
        transcendentals=0,
    )
    feature_spec = pl.BlockSpec((1, CHUNK), lambda i, half, *_: (0, half_of(half) * CHUNKS + i))
    weight_spec = pl.BlockSpec((CHUNK, width), lambda i, half, *_: (half_of(half) * CHUNKS + i, 0))
    normed_spec = pl.BlockSpec((tokens, CHUNK), lambda i, *_: (0, i))
    state_specs = [
        pl.BlockSpec(state_block, lambda i, *_: (0, i, 0, 0)),
        inverse_spec,
        feature_spec,
        feature_spec,
    ]
    sums_shape = jax.ShapeDtypeStruct((tokens, width), f32)
    top_shape = jax.ShapeDtypeStruct((1, width), f32)
    value_shape = jax.ShapeDtypeStruct((tokens, LANES), f32)

    with jax.named_scope("logits"):
        normed, value_lanes = pl.pallas_call(
            normed_kernel,
            out_shape=[jax.ShapeDtypeStruct((tokens, HALF), bf16), value_shape],
            grid_spec=pltpu.PrefetchScalarGridSpec(
                num_scalar_prefetch=1,
                grid=(CHUNKS,),
                in_specs=state_specs,
                out_specs=[normed_spec, whole(value_shape.shape)],
                scratch_shapes=[pltpu.VMEM((tokens, LANES), f32)],
            ),
            compiler_params=roomy,
            cost_estimate=pl.CostEstimate(
                flops=8 * tokens * HALF, bytes_accessed=4 * tokens * HALF, transcendentals=0
            ),
        )(core_scalar, mine, mine, gain_row, value_row)

        def head(weight):
            return pl.pallas_call(
                head_kernel,
                out_shape=[sums_shape, top_shape],
                grid_spec=pltpu.PrefetchScalarGridSpec(
                    num_scalar_prefetch=1,
                    grid=(CHUNKS,),
                    in_specs=[normed_spec, weight_spec],
                    out_specs=[whole(sums_shape.shape), whole(top_shape.shape)],
                ),
                compiler_params=roomy,
                cost_estimate=logits_cost,
            )(core_scalar, normed, weight)

        critic_sums, critic_top = head(critic_weight)
        policy_sums, policy_top = head(policy_weight)
        extra_in = [critic_sums, policy_sums, value_lanes, critic_top, policy_top, info]
        out_shape = [
            jax.ShapeDtypeStruct((tokens, 2 * width), f32),
            jax.ShapeDtypeStruct((mp_size, 8, tokens), f32),
            jax.ShapeDtypeStruct((8, tokens), f32),
        ]
        powers, totals, own_rows = pl.pallas_call(
            totals_kernel,
            out_shape=out_shape,
            grid_spec=pltpu.PrefetchScalarGridSpec(
                num_scalar_prefetch=2,
                grid=(CHUNKS,),
                in_specs=state_specs
                + [weight_spec] * 2
                + [whole(array.shape) for array in extra_in],
                out_specs=[whole(shape.shape) for shape in out_shape],
                scratch_shapes=[
                    pltpu.VMEM((tokens, LANES), f32),
                    pltpu.VMEM((1, width), f32),
                    pltpu.VMEM((tokens, CHUNK), bf16),
                    pltpu.VMEM((tokens, LANES), f32),
                ],
            ),
            compiler_params=roomy,
            cost_estimate=logits_cost,
        )(
            far_scalar,
            block_scalar,
            other,
            other,
            gain_row,
            value_row,
            critic_weight,
            policy_weight,
            *extra_in,
        )

    with jax.named_scope("totals"):
        totals, tile_is_row, share_is_row = lax.optimization_barrier(
            (totals, tile_is_row, share_is_row)
        )
        totals = lax.all_to_all(totals, "mp", 0, 0)
        totals = pl.pallas_call(
            merge_kernel,
            out_shape=jax.ShapeDtypeStruct((dp_size, 8, tokens), f32),
            compiler_params=roomy,
        )(totals)
        totals = lax.all_to_all(totals, "dp", 0, 0)

    matmul_cost = pl.CostEstimate(
        flops=2 * tokens * HALF * 2 * width,
        bytes_accessed=2 * (2 * HALF * width + 2 * tokens * HALF),
        transcendentals=0,
    )
    part_shape = (dp_size, TILES + TILES // rows, rows, LANES)

    def part(which, states, extra, with_grads):
        def chunk(i):
            return jnp.minimum(i, CHUNKS - 1)

        weight_spec = pl.BlockSpec(
            (CHUNK, width), lambda i, half, _: (half_of(half) * CHUNKS + chunk(i), 0)
        )
        out_shape = [jax.ShapeDtypeStruct(part_shape, f32)]
        out_specs = [pl.BlockSpec(state_block, lambda i, *_: (0, i, 0, 0))]
        if with_grads:
            out_shape += [
                jax.ShapeDtypeStruct((tokens, 2 * width), bf16),
                jax.ShapeDtypeStruct((tokens, LANES), f32),
            ]
            out_specs += [whole((tokens, 2 * width)), whole((tokens, LANES))]
        return pl.pallas_call(
            functools.partial(part_kernel, with_grads),
            out_shape=out_shape,
            grid_spec=pltpu.PrefetchScalarGridSpec(
                num_scalar_prefetch=2,
                grid=(CHUNKS + 1,),
                in_specs=[whole(array.shape) for array in extra]
                + [
                    pl.BlockSpec(state_block, lambda i, *_: (0, chunk(i), 0, 0)),
                    inverse_spec,
                    weight_spec,
                    weight_spec,
                ],
                out_specs=out_specs,
                scratch_shapes=[pltpu.VMEM((TILES, LANES), f32)]
                + [pltpu.VMEM((tokens, LANES), f32)] * 2,
            ),
            compiler_params=roomy,
            cost_estimate=matmul_cost,
        )(which, block_scalar, *extra, states, states, critic_weight, policy_weight)

    with jax.named_scope("reduce"):
        part_other, grads, column = part(
            far_scalar, other, [totals, own_rows, info, powers], True
        )
        arrived = swap(part_other.astype(f16))
        (part_mine,) = part(core_scalar, mine, [grads, column], False)
        joined = (part_mine + arrived.astype(f32)).astype(f16)
        lines = exchange(joined.reshape((side, side) + part_shape[1:]), False)

    def weight_grads(which, states, grads, earlier):
        far = bool(earlier)
        out_shape = [
            jax.ShapeDtypeStruct((D, width), bf16),
            jax.ShapeDtypeStruct((1, D), f32),
        ]
        out_specs = [
            pl.BlockSpec((CHUNK, width), lambda i, half: (half_of(half) * CHUNKS + i, 0)),
            pl.BlockSpec((1, CHUNK), lambda i, half: (0, half_of(half) * CHUNKS + i)),
        ]
        if not far:
            out_shape += [jax.ShapeDtypeStruct((TILES, LANES), f32)]
            out_specs += [pl.BlockSpec((CHUNK_TILES, LANES), lambda i, half: (i, 0))]
        return pl.pallas_call(
            functools.partial(weights_kernel, far),
            out_shape=out_shape,
            grid_spec=pltpu.PrefetchScalarGridSpec(
                num_scalar_prefetch=1,
                grid=(CHUNKS,),
                in_specs=[
                    pl.BlockSpec(state_block, lambda i, half: (0, i, 0, 0)),
                    inverse_spec,
                    pl.BlockSpec((1, CHUNK), lambda i, half: (0, half_of(half) * CHUNKS + i)),
                    pl.BlockSpec((tokens, width), lambda i, half: (0, 0)),
                    whole((tokens, LANES)),
                ]
                + [pl.BlockSpec(memory_space=pl.ANY)] * len(earlier),
                out_specs=out_specs,
                scratch_shapes=[pltpu.VMEM((tokens, CHUNK), bf16)]
                + [pltpu.VMEM((tokens, LANES), f32)] * 2,
            ),
            input_output_aliases={6: 0, 7: 1} if far else {},
            compiler_params=roomy,
            cost_estimate=pl.CostEstimate(
                flops=2 * tokens * HALF * width,
                bytes_accessed=2 * (HALF * width + 2 * tokens * HALF),
                transcendentals=0,
            ),
        )(which, states, states, gain_row, grads, column, *earlier)

    with jax.named_scope("lines"):
        lines, grads = lax.optimization_barrier((lines, grads))
        line = pack(jnp.sum(lines.astype(f32), axis=0), tile_is_row)
        parts = exchange(line, True)
        grad_critic, grad_value, extra = weight_grads(core_scalar, mine, grads, [])
        token = lax.dynamic_slice(column, (block_index, 0), (1, LANES))
        state_row = lax.dynamic_slice_in_dim(hidden_state, mp_index, 1, 0).reshape(
            2 * TILES, LANES
        )
        parts, grads, extra, token, state_row = lax.optimization_barrier(
            (parts, grads, extra, token, state_row)
        )

    with jax.named_scope("chips"):
        block = jnp.sum(unpack(parts, tile_is_row), axis=0).reshape(-1, LANES)
        shares = pl.pallas_call(
            split_kernel,
            out_shape=jax.ShapeDtypeStruct((chip_count, 3 * TILES, LANES), f32),
            compiler_params=roomy,
        )(block)
        shares = lax.all_to_all(
            pack(shares, share_is_row), "mp", 0, 0, axis_index_groups=chip_groups
        )
        far_extra = swap(extra)
        grad_critic, grad_value = weight_grads(
            far_scalar, other, grads, [grad_critic, grad_value]
        )
        shares, far_extra, grad_value = lax.optimization_barrier((shares, far_extra, grad_value))
        own = jnp.sum(unpack(shares, share_is_row), axis=0)
        far = swap(own)

    with jax.named_scope("finish"):
        smem = pl.BlockSpec(memory_space=pltpu.SMEM)
        vmem = pl.BlockSpec(memory_space=pltpu.VMEM)
        grad_hidden, grad_gain = pl.pallas_call(
            finish_kernel,
            out_shape=[
                jax.ShapeDtypeStruct((1, D), bf16),
                jax.ShapeDtypeStruct((2 * TILES, LANES), f32),
            ],
            in_specs=[smem] + [vmem] * 8,
            compiler_params=roomy,
        )(
            core_scalar,
            token,
            own,
            far,
            extra,
            far_extra,
            state_row,
            norm_gain.reshape(2 * TILES, LANES),
            value_weight.reshape(2 * TILES, LANES),
        )
    return (grad_hidden, grad_gain.reshape(D), grad_critic, grad_value.reshape(D))


def solution(mesh):
    placed = (
        P("dp", None),
        P(),
        P(None, ("dp", "mp")),
        P(None, ("dp", "mp")),
        P(),
        P(),
        P(),
        P(),
        P(),
    )
    return jax.shard_map(
        body,
        mesh=mesh,
        in_specs=placed,
        out_specs=(P(("dp", "mp"), None), P(), P(None, ("dp", "mp")), P()),
        check_vma=False,
    )
```

time: 142 us -> 136 us (0.958)
  local copies, waits for them, and re-layouts: 12.4 us -> 3.19 us
  waiting for transfers between devices: 18 us -> 8.95 us
  blocking collectives: 60.1 us -> 65.8 us
  starting transfers between devices: 16.6 us -> 21.8 us
  Pallas kernels: 28.6 us -> 30.4 us
    all_to_all x2, blocking collectives: 21.7 us -> 38.5 us  [exchange(): lax.all_to_all(flat, ('dp', 'mp'), 0, 0, axis_index_groups=axis_groups(tu...]
    all_to_all x2 -> x1, waiting for transfers between devices: 15.6 us -> 0.92 us  [exchange(): lax.all_to_all(flat, ('dp', 'mp'), 0, 0, axis_index_groups=axis_groups(tu...]
    all_to_all x1 -> x0, blocking collectives: 11.1 us -> none  [body(): lax.all_to_all(shares.astype(f16), 'mp', 0, 0, axis_index_groups=chip_gro...]
    unnamed x26 -> x18, local copies, waits for them, and re-layouts: 9.73 us -> 1.64 us
    ppermute x0 -> x3, waiting for transfers between devices: none -> 6.07 us  [shift(): return lax.ppermute(array, ('dp', 'mp'), moves)]
    all_to_all x2 -> x1, starting transfers between devices: 8.42 us -> 3.65 us  [exchange(): lax.all_to_all(flat, ('dp', 'mp'), 0, 0, axis_index_groups=axis_groups(tu...]
    ppermute x0 -> x3, starting transfers between devices: none -> 4.67 us  [shift(): return lax.ppermute(array, ('dp', 'mp'), moves)]
    all_to_all x0 -> x1, starting transfers between devices: none -> 3.39 us  [body(): lax.all_to_all(pack(shares, share_is_row), 'mp', 0, 0, axis_index_groups=...]
  transfers between devices with their start and end apart: 6 -> 9, of which waited for: 5 -> 7; matrix products, arithmetic and copies ran while one was open for 1% -> 1% of each run, Pallas kernels for 12% -> 14%
where the time goes in v3:
time: 136 us; the launch traced here: 135 us
  blocking collectives  65.8 us (48%)
  Pallas kernels  30.4 us (22%)
  starting transfers between devices  21.8 us (16%)
  waiting for transfers between devices  8.95 us (7%)
  other arithmetic  3.85 us (3%)
  local copies, waits for them, and re-layouts  3.19 us (2%)
    all_to_all x2, blocking collectives, exchange(): lax.all_to_all(flat, ('dp', 'mp'), 0, 0, axis_index_groups=axis_groups(tu...  38.5 us
    all_to_all x1, blocking collectives, body(): totals = lax.all_to_all(totals, 'mp', 0, 0)  17.6 us
    pallas_call x2, Pallas kernels, weight_grads(): pl.pallas_call(functools.partial(weights_kernel, far), out_shape=out_shap...  10.6 us
    ppermute x4, starting transfers between devices, swap(): return lax.ppermute(array, 'mp', core_swap)  10.1 us
    all_to_all x1, blocking collectives, body(): totals = lax.all_to_all(totals, 'dp', 0, 0)  9.79 us
    pallas_call x2, Pallas kernels, part(): pl.pallas_call(functools.partial(part_kernel, with_grads), out_shape=out_...  8.35 us
    ppermute x3, waiting for transfers between devices, shift(): return lax.ppermute(array, ('dp', 'mp'), moves)  6.07 us
    pallas_call x1, Pallas kernels, body(): pl.pallas_call(totals_kernel, out_shape=out_shape, grid_spec=pltpu.Prefet...  4.91 us
  transfers between devices with their start and end apart: 9, of which 7 were waited for; matrix products, arithmetic and copies ran while one was open for 1% of the time, Pallas kernels for 14%

profile of v3, /device:TPU:1, one launch (start us, length us, event | category | flops | bytes accessed | tf_op | source)
XLA Modules:
  0.0 135.0 jit_solution(6726688003705360654)
XLA Ops:
  0.6 0.0 copy-start.2
  0.7 0.9 copy-done.2
  1.6 0.2 norm.1
  1.8 3.6 %collective-permute-start = (bf16[33,16,128]{2,1,0:T(8,128)(2,1)S(1)}, bf16[33,16,128]{2,1,0:T(8,128)(2,1)S(1)}, u32[]{:S(2)}, u32[]{:S(2)}) collective-permute-start(bf16[33,16,128]{2,1,0:T(8,128)(2,1)S(1)} %norm.1), channel_id=1, source_target_pairs={{0,192},{1,49},{2,194},{3,51},{4,196},{5,53},{6,198},{7,55},{8,200... | collective-permute-start | bytes 405512 | tf_op jit(solution)/shard_map/gather/ppermute | solution.py:536
  5.4 0.3 collective-permute-start.1
  5.8 0.7 collective-permute-start.2
  6.4 2.4 %collective-permute-done = bf16[33,16,128]{2,1,0:T(8,128)(2,1)S(1)} collective-permute-done((bf16[33,16,128]{2,1,0:T(8,128)(2,1)S(1)}, bf16[33,16,128]{2,1,0:T(8,128)(2,1)S(1)}, u32[]{:S(2)}, u32[]{:S(2)}) %collective-permute-start) | collective-permute-done | bytes 135200 | tf_op jit(solution)/shard_map/gather/ppermute | solution.py:536
  8.8 2.3 %collective-permute-done.1 = bf16[33,16,128]{2,1,0:T(8,128)(2,1)S(1)} collective-permute-done((bf16[33,16,128]{2,1,0:T(8,128)(2,1)S(1)}, bf16[33,16,128]{2,1,0:T(8,128)(2,1)S(1)}, u32[]{:S(2)}, u32[]{:S(2)}) %collective-permute-start.1) | collective-permute-done | bytes 135200 | tf_op jit(solution)/shard_map/gather/ppermute | solution.py:536
  11.1 1.4 %collective-permute-done.2 = bf16[33,16,128]{2,1,0:T(8,128)(2,1)S(1)} collective-permute-done((bf16[33,16,128]{2,1,0:T(8,128)(2,1)S(1)}, bf16[33,16,128]{2,1,0:T(8,128)(2,1)S(1)}, u32[]{:S(2)}, u32[]{:S(2)}) %collective-permute-start.2) | collective-permute-done | bytes 135200 | tf_op jit(solution)/shard_map/gather/ppermute | solution.py:536
  12.5 0.1 pad_maximum_fusion
  12.6 0.3 broadcast_in_dim.35
  12.9 0.0 copy-start.3
  12.9 0.0 copy-start.4
  12.9 0.0 copy-start.5
  12.9 0.0 copy-start.6
  12.9 0.0 copy-start.7
  12.9 0.0 copy-start.8
  12.9 19.7 %all_to_all.30 = bf16[4,2112,128]{2,1,0:T(8,128)(2,1)S(1)} all-to-all(bf16[4,2112,128]{2,1,0:T(8,128)(2,1)S(1)} %broadcast_in_dim.35), channel_id=1, replica_groups={{0,16,32,48},{64,80,96,112},{128,144,160,176},{192,208,224,240},{2,18,3..., dimensions={0} | all-to-all | bytes 4325376 | tf_op jit(solution)/shard_map/gather/all_to_all | solution.py:540
  32.6 3.2 %collective-permute-start.3 = (bf16[16,33,16,128]{3,2,1,0:T(8,128)(2,1)S(1)}, bf16[16,33,16,128]{3,2,1,0:T(8,128)(2,1)}, u32[]{:S(2)}, u32[]{:S(2)}) collective-permute-start(bf16[16,33,16,128]{3,2,1,0:T(8,128)(2,1)S(1)} %bitcast.25), channel_id=1, source_target_pairs={{0,1},{1,0},{2,3},{3,2},{4,5},{5,4},{6,7},{7,6},{8,9},{9,8},{10,11... | collective-permute-start | bytes 6488072 | tf_op jit(solution)/shard_map/gather/ppermute | solution.py:506
  35.8 0.0 copy-done.3
  35.8 0.0 copy-done.4
  35.8 0.0 copy-done.5
  35.8 0.0 copy-done.6
  35.9 0.0 copy-done.7
  35.9 0.0 copy-done.8
  35.9 0.0 copy-start
  36.0 2.0 %logits.4 = (bf16[256,4096]{1,0:T(8,128)(2,1)S(1)}, f32[256,128]{1,0:T(8,128)S(1)}) custom-call(s32[1]{0:T(128)} %bitcast.core_ref, bf16[16,33,16,128]{3,2,1,0:T(8,128)(2,1)S(1)} %bitcast.26, bf16[16,33,16,128]{3,2,1,0:T(8,128)(2,1)S(1)} %bitcast.27, bf16[1,8192]{1,0:T(2,128)(2,1)S(1)} %reshape.74.gain_ref, bf16[1,8192]{1,0:T(2,128)(2,1)S(1)} %reshape.75.value_ref), custom_call_target="tpu_custom_call" | custom-call | flops 8388608 | bytes 4194304 | tf_op jit(solution)/shard_map/logits/pallas_call | solution.py:603
  38.0 0.1 copy-done
  38.1 0.0 copy-start.1
  38.1 1.7 %logits.5 = (f32[256,256]{1,0:T(8,128)S(1)}, f32[1,256]{1,0:T(1,128)S(1)}) custom-call(s32[1]{0:T(128)} %bitcast.core_ref, bf16[256,4096]{1,0:T(8,128)(2,1)S(1)} %get-tuple-element.36.normed_ref, bf16[8192,256]{1,0:T(8,128)(2,1)S(1)} %copy-done), custom_call_target="tpu_custom_call" | custom-call | flops 536870912 | bytes 4194304 | tf_op jit(solution)/shard_map/logits/pallas_call | solution.py:620
  39.8 0.5 copy-done.1
  40.3 1.7 %logits.6 = (f32[256,256]{1,0:T(8,128)S(1)}, f32[1,256]{1,0:T(1,128)S(1)}) custom-call(s32[1]{0:T(128)} %bitcast.core_ref, bf16[256,4096]{1,0:T(8,128)(2,1)S(1)} %get-tuple-element.36.normed_ref, bf16[8192,256]{1,0:T(8,128)(2,1)S(1)} %copy-done.1), custom_call_target="tpu_custom_call" | custom-call | flops 536870912 | bytes 4194304 | tf_op jit(solution)/shard_map/logits/pallas_call | solution.py:620
  42.0 0.0 collective-permute-done.3.state_ref.inverse_ref.refs_4_.refs_5_
  42.0 4.9 %logits.7 = (f32[256,512]{1,0:T(8,128)S(1)}, f32[16,8,256]{2,1,0:T(8,128)S(1)}, f32[8,256]{1,0:T(8,128)S(1)}) custom-call(s32[1]{0:T(128)} %bitcast.1.core_ref, s32[1]{0:T(128)} %bitcast.2.block_ref, bf16[16,33,16,128]{3,2,1,0:T(8,128)(2,1)} %collective-permute-done.3.state_ref.inverse_ref.refs_4_.refs_5_, ...), custom_call_target="tpu_custom_call" | custom-call | flops 536870912 | bytes 4194304 | tf_op jit(solution)/shard_map/logits/pallas_call | solution.py:641
  46.9 0.1 broadcast_in_dim.36
  47.0 0.1 broadcast_in_dim.37
  47.1 17.6 %all_to_all.31.parts_ref = f32[16,8,256]{2,1,0:T(8,128)S(1)} all-to-all(f32[16,8,256]{2,1,0:T(8,128)S(1)} %get-tuple-element.44), channel_id=1, replica_groups=mesh['dp'=16,'mp'=16] {'mp'}, dimensions={0} | all-to-all | bytes 262144 | tf_op jit(solution)/shard_map/totals/all_to_all | solution.py:676
  64.7 0.1 totals.1
  64.7 9.8 %all_to_all.32.refs_0_ = f32[16,8,256]{2,1,0:T(8,128)S(1)} all-to-all(f32[16,8,256]{2,1,0:T(8,128)S(1)} %totals.1), channel_id=1, replica_groups=mesh['dp'=16,'mp'=16] {'dp'}, dimensions={0} | all-to-all | bytes 262144 | tf_op jit(solution)/shard_map/totals/all_to_all | solution.py:682
  74.5 5.0 %reduce.4 = (f32[16,34,16,128]{3,2,1,0:T(8,128)S(1)}, bf16[256,512]{1,0:T(8,128)(2,1)S(1)}, f32[256,128]{1,0:T(8,128)S(1)}) custom-call(s32[1]{0:T(128)} %bitcast.1.core_ref, s32[1]{0:T(128)} %bitcast.2.block_ref, f32[16,8,256]{2,1,0:T(8,128)S(1)} %all_to_all.32.refs_0_, f32[8,256]{1,0:T(8,128)S(1)} %get-tuple-element.45.refs_1_, ...), custom_call_target="tpu_custom_call" | custom-call | flops 1073741824 | bytes 8388608 | tf_op jit(solution)/shard_map/reduce/pallas_call | solution.py:706
  79.5 0.3 convert_element_type.29
  79.8 0.9 collective-permute-start.4
  80.7 3.4 %reduce.5 = f32[16,34,16,128]{3,2,1,0:T(8,128)S(1)} custom-call(s32[1]{0:T(128)} %bitcast.core_ref, s32[1]{0:T(128)} %bitcast.2.block_ref, bf16[256,512]{1,0:T(8,128)(2,1)S(1)} %get-tuple-element.57.refs_0_.grads_ref, f32[256,128]{1,0:T(8,128)S(1)} %get-tuple-element.48.refs_1_.column_ref, bf16[16,33,16,128]{3,2,1,0:T(8,128)(2,1)S(1)} %bitcast.28, ...), custom_call_target="tpu_custom_call" | custom-call | flops 1073741824 | bytes 8388608 | tf_op jit(solution)/shard_map/reduce/pallas_call | solution.py:706
  84.1 0.6 collective-permute-done.4
  84.7 0.6 add_convert_fusion
  85.3 18.8 %all_to_all.33 = f16[4,2176,128]{2,1,0:T(8,128)(2,1)S(1)} all-to-all(f16[4,2176,128]{2,1,0:T(8,128)(2,1)S(1)} %bitcast.37), channel_id=1, replica_groups={{0,64,128,192},{16,80,144,208},{32,96,160,224},{48,112,176,240},{2,66,1..., dimensions={0} | all-to-all | bytes 4456448 | tf_op jit(solution)/shard_map/reduce/all_to_all | solution.py:540
  104.1 0.3 convert_reduce_fusion
  104.4 1.1 fusion.2
  105.5 3.7 %all-to-all-start.4 = ((f16[4,544,128]{2,1,0:T(8,128)(2,1)}), f16[4,544,128]{2,1,0:T(8,128)(2,1)S(1)}, u32[]{:S(2)}, u32[]{:S(2)}) async-start(f16[4,544,128]{2,1,0:T(8,128)(2,1)} %fusion.2), calls=%async_computation.4 | async-start | bytes 1114112 | tf_op jit(solution)/shard_map/lines/all_to_all | solution.py:540
  109.1 1.0 dynamic-slice_reduce_fusion
  110.2 4.9 %lines.1 = (bf16[8192,256]{1,0:T(8,128)(2,1)}, f32[1,8192]{1,0:T(1,128)}, f32[32,128]{1,0:T(8,128)S(1)}) custom-call(s32[1]{0:T(128)} %bitcast.core_ref, bf16[16,33,16,128]{3,2,1,0:T(8,128)(2,1)S(1)} %bitcast.30, bf16[16,33,16,128]{3,2,1,0:T(8,128)(2,1)S(1)} %bitcast.31, bf16[1,8192]{1,0:T(2,128)(2,1)S(1)} %reshape.74.gain_ref, ...), custom_call_target="tpu_custom_call" | custom-call | flops 536870912 | bytes 6291456 | tf_op jit(solution)/shard_map/lines/pallas_call | solution.py:749
  115.1 0.9 all-to-all-done.4
  116.0 0.6 fusion.5
  116.6 0.1 chips.2
  116.7 0.8 fusion.8
  117.5 3.4 %all-to-all-start.5 = ((f16[8,96,128]{2,1,0:T(8,128)(2,1)}), f16[8,96,128]{2,1,0:T(8,128)(2,1)S(1)}, u32[]{:S(2)}, u32[]{:S(2)}) async-start(f16[8,96,128]{2,1,0:T(8,128)(2,1)} %fusion.8), calls=%async_computation.5 | async-start | bytes 393216 | tf_op jit(solution)/shard_map/chips/all_to_all | solution.py:796
  120.9 2.5 %collective-permute-start.5 = (f32[32,128]{1,0:T(8,128)S(1)}, f32[32,128]{1,0:T(8,128)S(1)}, u32[]{:S(2)}, u32[]{:S(2)}) collective-permute-start(f32[32,128]{1,0:T(8,128)S(1)} %get-tuple-element.56.own_extra_ref), channel_id=1, source_target_pairs={{0,1},{1,0},{2,3},{3,2},{4,5},{5,4},{6,7},{7,6},{8,9},{9,8},{10,11... | collective-permute-start | bytes 49160 | tf_op jit(solution)/shard_map/chips/ppermute | solution.py:506
  123.3 5.6 %chips.3 = (bf16[8192,256]{1,0:T(8,128)(2,1)}, f32[1,8192]{1,0:T(1,128)}) custom-call(s32[1]{0:T(128)} %bitcast.1.core_ref, bf16[16,33,16,128]{3,2,1,0:T(8,128)(2,1)} %collective-permute-done.3.state_ref.inverse_ref.refs_4_.refs_5_, ...), custom_call_target="tpu_custom_call", output_to_operand_aliasing={{0}: (6, {}), {1}: (7, {})} | custom-call | flops 536870912 | bytes 6291456 | tf_op jit(solution)/shard_map/chips/pallas_call | solution.py:749
  128.9 0.0 collective-permute-done.5.far_extra_ref
  128.9 0.5 all-to-all-done.5
  129.4 0.2 fusion.11.own_ref
  129.6 3.6 %collective-permute-start.6 = (f32[96,128]{1,0:T(8,128)S(1)}, f32[96,128]{1,0:T(8,128)S(1)}, u32[]{:S(2)}, u32[]{:S(2)}) collective-permute-start(f32[96,128]{1,0:T(8,128)S(1)} %fusion.11.own_ref), channel_id=1, source_target_pairs={{0,1},{1,0},{2,3},{3,2},{4,5},{5,4},{6,7},{7,6},{8,9},{9,8},{10,11... | collective-permute-start | bytes 147464 | tf_op jit(solution)/shard_map/chips/ppermute | solution.py:506
  133.2 0.9 collective-permute-done.6.far_ref
  134.1 0.9 finish.1
  (7 shorter events, 0.1 us)
Async XLA Ops:
  0.6 1.0 copy-start.2
  1.8 7.0 %collective-permute-start = (bf16[33,16,128]{2,1,0:T(8,128)(2,1)S(1)}, bf16[33,16,128]{2,1,0:T(8,128)(2,1)S(1)}, u32[]{:S(2)}, u32[]{:S(2)}) collective-permute-start(bf16[33,16,128]{2,1,0:T(8,128)(2,1)S(1)} %norm.1), channel_id=1, source_target_pairs={{0,192},{1,49},{2,194},{3,51},{4,196},{5,53},{6,198},{7,55},{8,200... | collective-permute-start | bytes 405512 | tf_op jit(solution)/shard_map/gather/ppermute | solution.py:536
  5.4 5.7 %collective-permute-start.1 = (bf16[33,16,128]{2,1,0:T(8,128)(2,1)S(1)}, bf16[33,16,128]{2,1,0:T(8,128)(2,1)S(1)}, u32[]{:S(2)}, u32[]{:S(2)}) collective-permute-start(bf16[33,16,128]{2,1,0:T(8,128)(2,1)S(1)} %norm.1), channel_id=1, source_target_pairs={{0,128},{1,33},{2,130},{3,35},{4,132},{5,37},{6,134},{7,39},{8,136... | collective-permute-start | bytes 405512 | tf_op jit(solution)/shard_map/gather/ppermute | solution.py:536
  5.8 6.8 %collective-permute-start.2 = (bf16[33,16,128]{2,1,0:T(8,128)(2,1)S(1)}, bf16[33,16,128]{2,1,0:T(8,128)(2,1)S(1)}, u32[]{:S(2)}, u32[]{:S(2)}) collective-permute-start(bf16[33,16,128]{2,1,0:T(8,128)(2,1)S(1)} %norm.1), channel_id=1, source_target_pairs={{0,64},{1,17},{2,66},{3,19},{4,68},{5,21},{6,70},{7,23},{8,72},{9,... | collective-permute-start | bytes 405512 | tf_op jit(solution)/shard_map/gather/ppermute | solution.py:536
  12.9 22.9 %copy-start.3 = (bf16[8192]{0:T(1024)(128)(2,1)S(1)}, bf16[8192]{0:T(1024)(128)(2,1)}, u32[]{:S(2)}) copy-start(bf16[8192]{0:T(1024)(128)(2,1)} %param.10) | copy-start | bytes 49156
  12.9 22.9 %copy-start.4 = (bf16[8192]{0:T(1024)(128)(2,1)S(1)}, bf16[8192]{0:T(1024)(128)(2,1)}, u32[]{:S(2)}) copy-start(bf16[8192]{0:T(1024)(128)(2,1)} %param.13) | copy-start | bytes 49156
  12.9 22.9 %copy-start.5 = (s32[256]{0:T(256)S(1)}, s32[256]{0:T(256)}, u32[]{:S(2)}) copy-start(s32[256]{0:T(256)} %param.17) | copy-start | bytes 3076
  12.9 22.9 %copy-start.6 = (s32[256]{0:T(256)S(1)}, s32[256]{0:T(256)}, u32[]{:S(2)}) copy-start(s32[256]{0:T(256)} %param.14) | copy-start | bytes 3076
  12.9 22.9 %copy-start.7 = (s32[256]{0:T(256)S(1)}, s32[256]{0:T(256)}, u32[]{:S(2)}) copy-start(s32[256]{0:T(256)} %param.15) | copy-start | bytes 3076
  12.9 22.9 %copy-start.8 = (s32[256]{0:T(256)S(1)}, s32[256]{0:T(256)}, u32[]{:S(2)}) copy-start(s32[256]{0:T(256)} %param.16) | copy-start | bytes 3076
  32.6 9.4 %collective-permute-start.3 = (bf16[16,33,16,128]{3,2,1,0:T(8,128)(2,1)S(1)}, bf16[16,33,16,128]{3,2,1,0:T(8,128)(2,1)}, u32[]{:S(2)}, u32[]{:S(2)}) collective-permute-start(bf16[16,33,16,128]{3,2,1,0:T(8,128)(2,1)S(1)} %bitcast.25), channel_id=1, source_target_pairs={{0,1},{1,0},{2,3},{3,2},{4,5},{5,4},{6,7},{7,6},{8,9},{9,8},{10,11... | collective-permute-start | bytes 6488072 | tf_op jit(solution)/shard_map/gather/ppermute | solution.py:506
  35.9 2.2 %copy-start = (bf16[8192,256]{1,0:T(8,128)(2,1)S(1)}, bf16[8192,256]{1,0:T(8,128)(2,1)}, u32[]{:S(2)}) copy-start(bf16[8192,256]{1,0:T(8,128)(2,1)} %refs_4_.1) | copy-start | bytes 12582916
  38.1 2.2 %copy-start.1 = (bf16[8192,256]{1,0:T(8,128)(2,1)S(1)}, bf16[8192,256]{1,0:T(8,128)(2,1)}, u32[]{:S(2)}) copy-start(bf16[8192,256]{1,0:T(8,128)(2,1)} %refs_5_.1) | copy-start | bytes 12582916
  79.8 4.9 %collective-permute-start.4 = (f16[16,34,16,128]{3,2,1,0:T(8,128)(2,1)S(1)}, f16[16,34,16,128]{3,2,1,0:T(8,128)(2,1)S(1)}, u32[]{:S(2)}, u32[]{:S(2)}) collective-permute-start(f16[16,34,16,128]{3,2,1,0:T(8,128)(2,1)S(1)} %convert_element_type.29), channel_id=1, source_target_pairs={{0,1},{1,0},{2,3},{3,2},{4,5},{5,4},{6,7},{7,6},{8,9},{9,8},{10,11... | collective-permute-start | bytes 6684680 | tf_op jit(solution)/shard_map/reduce/ppermute | solution.py:506
  105.5 10.6 %all-to-all-start.4 = ((f16[4,544,128]{2,1,0:T(8,128)(2,1)}), f16[4,544,128]{2,1,0:T(8,128)(2,1)S(1)}, u32[]{:S(2)}, u32[]{:S(2)}) async-start(f16[4,544,128]{2,1,0:T(8,128)(2,1)} %fusion.2), calls=%async_computation.4 | async-start | bytes 1114112 | tf_op jit(solution)/shard_map/lines/all_to_all | solution.py:540
  117.5 12.0 %all-to-all-start.5 = ((f16[8,96,128]{2,1,0:T(8,128)(2,1)}), f16[8,96,128]{2,1,0:T(8,128)(2,1)S(1)}, u32[]{:S(2)}, u32[]{:S(2)}) async-start(f16[8,96,128]{2,1,0:T(8,128)(2,1)} %fusion.8), calls=%async_computation.5 | async-start | bytes 393216 | tf_op jit(solution)/shard_map/chips/all_to_all | solution.py:796
  120.9 8.1 %collective-permute-start.5 = (f32[32,128]{1,0:T(8,128)S(1)}, f32[32,128]{1,0:T(8,128)S(1)}, u32[]{:S(2)}, u32[]{:S(2)}) collective-permute-start(f32[32,128]{1,0:T(8,128)S(1)} %get-tuple-element.56.own_extra_ref), channel_id=1, source_target_pairs={{0,1},{1,0},{2,3},{3,2},{4,5},{5,4},{6,7},{7,6},{8,9},{9,8},{10,11... | collective-permute-start | bytes 49160 | tf_op jit(solution)/shard_map/chips/ppermute | solution.py:506
  129.6 4.5 %collective-permute-start.6 = (f32[96,128]{1,0:T(8,128)S(1)}, f32[96,128]{1,0:T(8,128)S(1)}, u32[]{:S(2)}, u32[]{:S(2)}) collective-permute-start(f32[96,128]{1,0:T(8,128)S(1)} %fusion.11.own_ref), channel_id=1, source_target_pairs={{0,1},{1,0},{2,3},{3,2},{4,5},{5,4},{6,7},{7,6},{8,9},{9,8},{10,11... | collective-permute-start | bytes 147464 | tf_op jit(solution)/shard_map/chips/ppermute | solution.py:506
